TPU v7x, 128 devices: a whole 4x4x4 slice. The times are simulated.
128 devices in a mesh: group: 4 (over z), expert: 32 (over y, x, core).
Axes of the slice: x: 4, y: 4, z: 4, core: 2. Of those that a mesh axis runs over, the one named last changes fastest.
Arguments:
- layer_input: bfloat16 [4096, 4096], P(('group', 'expert')), may hold values from -6 to 6
- out_grad: bfloat16 [4096, 4096], P(('group', 'expert')), may hold values from -6 to 6
- merged: bfloat16 [4096, 4096], P(('group', 'expert')), may hold values from -6 to 6
- head_weight: bfloat16 [4096, 4096], P('group', 'expert'), may hold values from -0.09375 to 0.09375
- merge_weight: bfloat16 [4096, 4096], P('expert', 'group'), may hold values from -0.09375 to 0.09375
- expert_in: bfloat16 [32, 1024, 4096], P('expert', None, 'group'), may hold values from -0.1875 to 0.1875
- expert_out: bfloat16 [32, 4096, 1024], P('expert', 'group'), may hold values from -0.09375 to 0.09375
- dispatched: bfloat16 [32, 1536, 1024], P('expert', 'group'), may hold values from -6 to 6
- expert_ids: int32 [16384, 2], P(('group', 'expert')), may hold values from 0 to 31, all different within a row; in each aligned block of 128 rows (0 to 127, 128 to 255, ...) at most 12 rows name the same one
- gate_values: bfloat16 [16384, 2], P(('group', 'expert')), may hold values from 0.049804688 to 1
Outputs:
- input_grad: bfloat16 [4096, 4096], P(('group', 'expert'))
- head_grad: float32 [4096, 4096], P('group', 'expert')
- merge_grad: float32 [4096, 4096], P('expert', 'group')
- expert_in_grad: float32 [32, 1024, 4096], P('expert', None, 'group')
- expert_out_grad: float32 [32, 4096, 1024], P('expert', 'group')
- gate_grad: bfloat16 [16384, 2], P(('group', 'expert'))
Inputs may be any that keep to these rules, and one draw needn't show every extreme that they name: `expert_ids`: each row names two different experts. Within each aligned block of 128 rows (the sub-tokens of one device) no expert is named more than 12 times, and in every draw some block names some expert exactly 12 times.
All inputs are finite; a program needn't handle non-finite values.
Results may differ from a plain program's by a relative error of at most 0.025.
Values may be sent and summed in bfloat16 or wider, within the bound.
A program may use at most 128 MiB of HBM per device.

v0:
```python
import jax
import jax.numpy as jnp
from jax import lax
from jax.sharding import PartitionSpec as P

DS = 1024
HEADS = 4


root_scale = 0.7978845608028654
cubic_term = 0.044715


def gelu_value(value):
    inner = root_scale * (value + cubic_term * value * value * value)
    return 0.5 * value * (1.0 + jnp.tanh(inner))


def gelu_slope(value):
    inner = root_scale * (value + cubic_term * value * value * value)
    tangent = jnp.tanh(inner)
    return 0.5 * (1.0 + tangent) + 0.5 * value * (1.0 - tangent * tangent) * root_scale * (
        1.0 + 3.0 * cubic_term * value * value
    )


def contract_first(left, right):
    return lax.dot_general(
        left, right, (((0,), (0,)), ((), ())), preferred_element_type=jnp.float32
    )


def contract_last(left, right):
    return lax.dot_general(
        left, right, (((1,), (1,)), ((), ())), preferred_element_type=jnp.float32
    )


def body(
    layer_input,
    out_grad,
    merged,
    head_weight,
    merge_weight,
    expert_in,
    expert_out,
    dispatched,
    expert_ids,
    gate_values,
):
    expert_count = lax.axis_size("expert")
    width = out_grad.shape[1]
    head_columns = lax.all_gather(head_weight, "group", axis=0, tiled=True)
    merge_rows = lax.all_gather(merge_weight, "group", axis=1, tiled=True)
    merged_columns = lax.all_to_all(merged, "expert", split_axis=1, concat_axis=0, tiled=True)
    piece = lax.all_gather(out_grad, "expert", axis=0, tiled=True)
    part = contract_last(piece, merge_rows)
    columns_grad = part
    local = merged_columns
    weight_grad = contract_first(local, piece)
    columns_grad, merge_partial = (columns_grad, weight_grad)
    merge_grad = lax.psum_scatter(
        merge_partial.astype(jnp.bfloat16), "group", scatter_dimension=1, tiled=True
    ).astype(jnp.float32)
    token_grad = lax.all_to_all(
        columns_grad.astype(jnp.bfloat16), "expert", split_axis=0, concat_axis=1, tiled=True
    )
    sub_count = token_grad.shape[0] * HEADS
    sub_grad = token_grad.reshape(sub_count, DS)
    expert_total = expert_count * expert_in.shape[0]
    send_rows = dispatched.shape[1] // expert_count
    flat_ids = expert_ids.reshape(-1)
    onehot = (flat_ids[:, None] == jnp.arange(expert_total, dtype=jnp.int32)[None, :]).astype(
        jnp.int32
    )
    ranks = jnp.sum(onehot * jnp.cumsum(onehot, axis=0), axis=1) - 1
    targets = flat_ids * send_rows + ranks
    placement_table = (
        jnp.arange(expert_total * send_rows, dtype=jnp.int32)[:, None] == targets[None, :]
    ).astype(jnp.bfloat16)
    repeated = jnp.repeat(sub_grad, 2, axis=0)
    outgoing = (
        jnp.dot(placement_table, repeated, preferred_element_type=jnp.float32)
        .astype(jnp.bfloat16)
        .reshape(expert_total, send_rows, DS)
    )
    outgoing_gates = (
        jnp.dot(placement_table, gate_values.reshape(-1), preferred_element_type=jnp.float32)
        .astype(jnp.bfloat16)
        .reshape(expert_total, send_rows)
    )
    arrived, arrived_gates = (
        lax.all_to_all(outgoing, "expert", split_axis=0, concat_axis=0, tiled=True),
        lax.all_to_all(outgoing_gates, "expert", split_axis=0, concat_axis=0, tiled=True),
    )
    arrived = arrived.reshape(-1, DS)
    arrived_gates = arrived_gates.reshape(-1)
    weight_in = expert_in[0]
    weight_out = expert_out[0]
    inputs_local = dispatched[0]
    combined = lax.all_gather(arrived, "group", axis=0, tiled=True)
    gates = lax.all_gather(arrived_gates, "group", axis=0, tiled=True)
    inputs = lax.all_gather(inputs_local, "group", axis=0, tiled=True)
    before = jnp.dot(inputs, weight_in, preferred_element_type=jnp.float32)
    hidden = gelu_value(before).astype(jnp.bfloat16)
    produced = jnp.dot(hidden, weight_out, preferred_element_type=jnp.float32)
    scaled = (gates.astype(jnp.float32)[:, None] * combined.astype(jnp.float32)).astype(
        jnp.bfloat16
    )
    hidden_grad = contract_last(scaled, weight_out)
    before_grad = (hidden_grad * gelu_slope(before)).astype(jnp.bfloat16)
    out_weight_grad = contract_first(hidden, scaled)
    in_grad = contract_first(inputs, before_grad)
    rows_part = contract_last(before_grad, weight_in)
    gate_part = jnp.sum(combined.astype(jnp.float32) * produced, axis=1)
    row_grads = rows_part
    gate_sums = gate_part
    in_grad, out_weight_grad, row_grads, gate_sums = (
        in_grad,
        out_weight_grad,
        row_grads,
        gate_sums,
    )
    row_sums, gate_totals = (
        lax.psum_scatter(
            row_grads.astype(jnp.bfloat16), "group", scatter_dimension=0, tiled=True
        ).astype(jnp.float32),
        lax.psum_scatter(
            gate_sums.astype(jnp.bfloat16), "group", scatter_dimension=0, tiled=True
        ).astype(jnp.float32),
    )
    back_rows = row_sums.astype(jnp.bfloat16).reshape(expert_total, send_rows, DS)
    back_gates = gate_totals.astype(jnp.bfloat16).reshape(expert_total, send_rows)
    returned, returned_gates = (
        lax.all_to_all(back_rows, "expert", split_axis=0, concat_axis=0, tiled=True),
        lax.all_to_all(back_gates, "expert", split_axis=0, concat_axis=0, tiled=True),
    )
    picked = contract_first(placement_table, returned.reshape(-1, DS)).reshape(sub_count, 2, DS)
    head_out_grad = (
        jnp.sum(gate_values.astype(jnp.float32)[:, :, None] * picked, axis=1)
        .astype(jnp.bfloat16)
        .reshape(-1, width)
    )
    gate_grad = (
        contract_first(placement_table, returned_gates.reshape(-1, 1))
        .astype(jnp.bfloat16)
        .reshape(sub_count, 2)
    )
    grad_columns = lax.all_to_all(head_out_grad, "expert", split_axis=1, concat_axis=0, tiled=True)
    local = grad_columns
    head_total = contract_first(lax.all_gather(layer_input, "expert", axis=0, tiled=True), local)
    local = grad_columns
    input_total = lax.psum_scatter(
        contract_last(local, head_columns).astype(jnp.bfloat16),
        "expert",
        scatter_dimension=0,
        tiled=True,
    )
    head_grad = lax.psum_scatter(
        head_total.astype(jnp.bfloat16), "group", scatter_dimension=0, tiled=True
    ).astype(jnp.float32)
    return (input_total, head_grad, merge_grad, in_grad[None], out_weight_grad[None], gate_grad)


def solution(mesh):
    placed = (
        P(("group", "expert"), None),
        P(("group", "expert"), None),
        P(("group", "expert"), None),
        P("group", "expert"),
        P("expert", "group"),
        P("expert", None, "group"),
        P("expert", "group", None),
        P("expert", "group", None),
        P(("group", "expert"), None),
        P(("group", "expert"), None),
    )
    return jax.shard_map(
        body,
        mesh=mesh,
        in_specs=placed,
        out_specs=(
            P(("group", "expert"), None),
            P("group", "expert"),
            P("expert", "group"),
            P("expert", None, "group"),
            P("expert", "group", None),
            P(("group", "expert"), None),
        ),
        check_vma=False,
    )
```

profile of v0, /device:TPU:1, one launch (start us, length us, event | category | flops | bytes accessed | tf_op | source)
XLA Modules:
  0.0 472.3 jit_solution(14261941816245214462)
XLA Ops:
  11.3 24.9 %all-gather.11.cloned.1.call-done = bf16[128,4096]{1,0:T(8,128)(2,1)} async-done(((bf16[128,1024]{1,0:T(8,128)(2,1)}), bf16[128,4096]{1,0:T(8,128)(2,1)}) %all-gather.11.cloned.1.call-update) | async-done | bytes 1048592 | tf_op jit(solution)/shard_map/all_gather | solution.py:54
  36.2 56.8 %all-gather.9.cloned.1.call-done = bf16[1024,4096]{1,0:T(8,128)(2,1)} async-done(((bf16[32,4096]{1,0:T(8,128)(2,1)}), bf16[1024,4096]{1,0:T(8,128)(2,1)}) %all-gather.9.cloned.1.call-update) | async-done | bytes 8388624 | tf_op jit(solution)/shard_map/all_gather | solution.py:56
  93.0 6.6 %convolution_convert_fusion.5 = bf16[1024,128]{1,0:T(8,128)(2,1)} fusion(bf16[1024,4096]{1,0:T(8,128)(2,1)} %all-gather.9.cloned.1.call-done, bf16[128,4096]{1,0:T(8,128)(2,1)} %all-gather.11.cloned.1.call-done), kind=kOutput, calls=%fused_computation.33 | convolution fusion | flops 1073872896 | bytes 9699328 | tf_op jit(solution)/shard_map/dot_general | solution.py:34
  105.3 8.7 %all-to-all-done.1 = bf16[32,32,128]{2,1,0:T(8,128)(2,1)S(1)} async-done(((bf16[32,32,128]{2,1,0:T(8,128)(2,1)}), bf16[32,32,128]{2,1,0:T(8,128)(2,1)S(1)}, u32[]{:S(2)}, u32[]{:S(2)}) %all-to-all-start.1) | async-done | bytes 262176 | tf_op jit(solution)/shard_map/all_to_all | solution.py:65
  117.3 20.9 %all_to_all.81 = bf16[32,12,1024]{2,1,0:T(8,128)(2,1)} all-to-all(bf16[32,12,1024]{2,1,0:T(8,128)(2,1)S(1)} %reshape.134), channel_id=1, replica_groups=mesh['group'=4,'expert'=32] {'expert'}, dimensions={0} | all-to-all | bytes 1572864 | tf_op jit(solution)/shard_map/all_to_all | solution.py:93
  141.3 10.4 %all_to_all.82 = bf16[32,1,12]{2,1,0:T(2,128)(2,1)S(1)} all-to-all(bf16[32,1,12]{2,1,0:T(2,128)(2,1)S(1)} %all_to_all.72), channel_id=1, replica_groups=mesh['group'=4,'expert'=32] {'expert'}, dimensions={0} | all-to-all | bytes 1536 | tf_op jit(solution)/shard_map/all_to_all | solution.py:94
  151.9 9.8 %all-gather.1 = bf16[4,1,384]{2,1,0:T(2,128)(2,1)S(1)} all-gather(bf16[1,1,384]{2,1,0:T(2,128)(2,1)S(1)} %reshape.141), channel_id=1, replica_groups=mesh['group'=4,'expert'=32] {'group'}, dimensions={0}, use_global_device_ids=true | all-gather | bytes 3840 | tf_op jit(solution)/shard_map/all_gather | solution.py:102
  161.8 7.3 %fusion.12 = f32[1536,1024]{1,0:T(8,128)} fusion(bf16[1,1536,1024]{2,1,0:T(8,128)(2,1)} %all-gather.19.cloned.1.call-done, bf16[1,1024,1024]{2,1,0:T(8,128)(2,1)S(1)} %copy-done), kind=kOutput, calls=%fused_computation.21 | convolution fusion | flops 3221225472 | bytes 11534336 | tf_op jit(solution)/shard_map/dot_general | solution.py:104
  169.0 9.1 %all-gather.13.cloned.1.call-done = bf16[1536,1024]{0,1:T(8,128)(2,1)} async-done(((bf16[384,1024]{0,1:T(8,128)(2,1)}), bf16[1536,1024]{0,1:T(8,128)(2,1)}) %all-gather.13.cloned.1.call-update) | async-done | bytes 3145744 | tf_op jit(solution)/shard_map/all_gather | solution.py:101
  178.1 9.9 %fusion.8 = bf16[1536,1024]{1,0:T(8,128)(2,1)S(1)} fusion(f32[1536,1024]{1,0:T(8,128)} %fusion.12, bf16[1536,1024]{0,1:T(8,128)(2,1)} %all-gather.13.cloned.1.call-done, f32[1536]{0:T(1024)S(1)} %reshape.143, bf16[1,1024,1024]{2,1,0:T(8,128)(2,1)} %param.16), kind=kOutput, calls=%fused_computation.13 | convolution fusion | flops 3255828480 | bytes 14686208 | tf_op jit(solution)/shard_map/dot_general | solution.py:34
  196.1 16.2 %all_to_all.83 = bf16[32,32,128]{2,0,1:T(8,128)(2,1)S(1)} all-to-all(bf16[32,32,128]{2,0,1:T(8,128)(2,1)S(1)} %copy_bitcast_fusion), channel_id=1, replica_groups=mesh['group'=4,'expert'=32] {'expert'}, dimensions={1} | all-to-all | bytes 524288 | tf_op jit(solution)/shard_map/all_to_all | solution.py:55
  212.3 5.7 %convolution_convert_fusion.1 = bf16[128,4096]{1,0:T(8,128)(2,1)} fusion(bf16[1024,128]{1,0:T(8,128)(2,1)S(1)} %bitcast.71, bf16[1024,4096]{1,0:T(8,128)(2,1)} %all-gather.9.cloned.1.call-done), kind=kOutput, calls=%fused_computation.15 | convolution fusion | flops 1074266112 | bytes 9699328 | tf_op jit(solution)/shard_map/dot_general | solution.py:28
  218.1 15.2 %reduce-scatter.5.cloned.1.call-done = bf16[384,1024]{1,0:T(8,128)(2,1)} async-done(((bf16[1536,1024]{1,0:T(8,128)(2,1)}), bf16[384,1024]{1,0:T(8,128)(2,1)}) %reduce-scatter.5.cloned.1.call-update) | async-done | bytes 786448 | tf_op jit(solution)/shard_map/reduce_scatter | solution.py:125
  235.4 7.5 %all-to-all-start.3 = ((bf16[32,12,1024]{2,1,0:T(8,128)(2,1)}), bf16[32,12,1024]{2,1,0:T(8,128)(2,1)S(1)}, u32[]{:S(2)}, u32[]{:S(2)}) async-start(bf16[32,12,1024]{2,1,0:T(8,128)(2,1)} %reshape.136), calls=%async_computation.4 | async-start | bytes 2097152 | tf_op jit(solution)/shard_map/all_to_all | solution.py:135
  243.1 19.8 %all-to-all-done.3 = bf16[32,12,1024]{2,1,0:T(8,128)(2,1)S(1)} async-done(((bf16[32,12,1024]{2,1,0:T(8,128)(2,1)}), bf16[32,12,1024]{2,1,0:T(8,128)(2,1)S(1)}, u32[]{:S(2)}, u32[]{:S(2)}) %all-to-all-start.3) | async-done | bytes 786464 | tf_op jit(solution)/shard_map/all_to_all | solution.py:135
  269.5 25.8 %all-gather.17.cloned.1.call-done = bf16[1024,4096]{1,0:T(8,128)(2,1)} async-done(((bf16[32,4096]{1,0:T(8,128)(2,1)}), bf16[1024,4096]{1,0:T(8,128)(2,1)}) %all-gather.17.cloned.1.call-update) | async-done | bytes 8388624 | tf_op jit(solution)/shard_map/all_gather | solution.py:151
  301.1 16.2 %all-gather.15.cloned.1.call-done = bf16[4096,128]{1,0:T(8,128)(2,1)} async-done(((bf16[1024,128]{1,0:T(8,128)(2,1)}), bf16[4096,128]{1,0:T(8,128)(2,1)}) %all-gather.15.cloned.1.call-update) | async-done | bytes 1048592 | tf_op jit(solution)/shard_map/all_gather | solution.py:53
  317.4 6.8 %convolution_convert_fusion = bf16[1024,4096]{1,0:T(8,128)(2,1)} fusion(bf16[1024,128]{1,0:T(8,128)(2,1)S(1)} %bitcast.70, bf16[4096,128]{1,0:T(8,128)(2,1)} %all-gather.15.cloned.1.call-done), kind=kOutput, calls=%fused_computation.4 | convolution fusion | flops 1077936128 | bytes 9699328 | tf_op jit(solution)/shard_map/dot_general | solution.py:34
  326.0 17.0 %reduce-scatter.11.cloned.1.call-done = bf16[128,1024]{1,0:T(8,128)(2,1)} async-done(((bf16[128,4096]{1,0:T(8,128)(2,1)}), bf16[128,1024]{1,0:T(8,128)(2,1)}) %reduce-scatter.11.cloned.1.call-update) | async-done | bytes 262160 | tf_op jit(solution)/shard_map/reduce_scatter | solution.py:62
  344.8 7.7 %fusion.1 = bf16[1536]{0:T(1024)(128)(2,1)S(1)} fusion(bf16[1536,1024]{0,1:T(8,128)(2,1)} %all-gather.13.cloned.1.call-done, bf16[1,1024,1024]{2,1,0:T(8,128)(2,1)S(1)} %copy-done.5, f32[1536,1024]{1,0:T(8,128)} %fusion.12), kind=kOutput, calls=%fused_computation.6 | convolution fusion | flops 3240098304 | bytes 11537408 | tf_op jit(solution)/shard_map/dot_general | solution.py:106
  352.5 7.5 %all-reduce = bf16[1536]{0:T(1024)(128)(2,1)S(1)} all-reduce(bf16[1536]{0:T(1024)(128)(2,1)S(1)} %fusion.1), channel_id=7, replica_groups=mesh['group'=4,'expert'=32] {'group'}, use_global_device_ids=true, to_apply=%region_9.10.clone | all-reduce | flops 1536 | bytes 6144
  360.9 10.1 %all-to-all-start.6 = ((bf16[32,1,12]{2,1,0:T(2,128)(2,1)}), bf16[32,1,12]{2,1,0:T(2,128)(2,1)S(1)}, u32[]{:S(2)}, u32[]{:S(2)}) async-start(bf16[32,1,12]{2,1,0:T(2,128)(2,1)} %all_to_all.73), calls=%async_computation.10 | async-start | bytes 32768 | tf_op jit(solution)/shard_map/all_to_all | solution.py:136
  371.0 10.3 %fusion.17 = f32[1,1024,1024]{2,1,0:T(8,128)} fusion(bf16[1536,1024]{0,1:T(8,128)(2,1)} %all-gather.13.cloned.1.call-done, f32[1536]{0:T(1024)S(1)} %reshape.143, f32[1536,1024]{1,0:T(8,128)} %fusion.12), kind=kOutput, calls=%fused_computation.24 | convolution fusion | flops 3240099840 | bytes 13637632 | tf_op jit(solution)/shard_map/dot_general | solution.py:28
  395.0 70.5 %reduce-scatter.7.cloned.1.call-done = bf16[32,4096]{1,0:T(8,128)(2,1)} async-done(((bf16[1024,4096]{1,0:T(8,128)(2,1)}), bf16[32,4096]{1,0:T(8,128)(2,1)}) %reduce-scatter.7.cloned.1.call-update) | async-done | bytes 262160 | tf_op jit(solution)/shard_map/reduce_scatter | solution.py:153
  (94 shorter events, 56.5 us)
Async XLA Ops:
  7.2 154.6 %copy-start = (bf16[1,1024,1024]{2,1,0:T(8,128)(2,1)S(1)}, bf16[1,1024,1024]{2,1,0:T(8,128)(2,1)}, u32[]{:S(2)}) copy-start(bf16[1,1024,1024]{2,1,0:T(8,128)(2,1)} %param.15) | copy-start | bytes 6291460
  7.2 29.0 %all-gather.11.cloned.1.call-start = ((), (), s32[]{:S(2)}) async-start(), calls=%async_computation.12 | async-start | bytes 1310720 | tf_op jit(solution)/shard_map/all_gather | solution.py:54
  7.9 85.1 %all-gather.9.cloned.1.call-start = ((), (), s32[]{:S(2)}) async-start(), calls=%async_computation.11 | async-start | bytes 8650752 | tf_op jit(solution)/shard_map/all_gather | solution.py:56
  8.7 153.1 %all-gather.19.cloned.1.call-start = ((), (), s32[]{:S(2)}) async-start(), calls=%async_computation.20 | async-start | bytes 3932160 | tf_op jit(solution)/shard_map/all_gather | solution.py:103
  99.6 14.4 %all-to-all-start.1 = ((bf16[32,32,128]{2,1,0:T(8,128)(2,1)}), bf16[32,32,128]{2,1,0:T(8,128)(2,1)S(1)}, u32[]{:S(2)}, u32[]{:S(2)}) async-start(bf16[32,32,128]{2,1,0:T(8,128)(2,1)} %bitcast.1), calls=%async_computation.1 | async-start | bytes 524288 | tf_op jit(solution)/shard_map/all_to_all | solution.py:65
  105.1 35.5 %copy-start.3 = (bf16[128,2]{0,1:T(2,128)(2,1)S(1)}, bf16[128,2]{0,1:T(2,128)(2,1)}, u32[]{:S(2)}) copy-start(bf16[128,2]{0,1:T(2,128)(2,1)} %param.19) | copy-start | bytes 1540
  105.1 73.0 %all-gather.13.cloned.1.call-start = ((), (), s32[]{:S(2)}) async-start(), calls=%async_computation.13 | async-start | bytes 3932160 | tf_op jit(solution)/shard_map/all_gather | solution.py:101
  140.6 92.6 %reduce-scatter.5.cloned.1.call-start = ((), (), s32[]{:S(2)}) async-start(), calls=%async_computation.14 | async-start | bytes 3932160 | tf_op jit(solution)/shard_map/reduce_scatter | solution.py:125
  188.0 1.7 copy-start.7
  189.7 6.4 %copy-start.2 = (bf16[32,4096]{1,0:T(8,128)(2,1)S(1)}, bf16[32,4096]{1,0:T(8,128)(2,1)}, u32[]{:S(2)}) copy-start(bf16[32,4096]{1,0:T(8,128)(2,1)} %param.12) | copy-start | bytes 786436
  194.7 100.7 %all-gather.17.cloned.1.call-start = ((), (), s32[]{:S(2)}) async-start(), calls=%async_computation.17 | async-start | bytes 8650752 | tf_op jit(solution)/shard_map/all_gather | solution.py:151
  195.2 122.1 %all-gather.15.cloned.1.call-start = ((), (), s32[]{:S(2)}) async-start(), calls=%async_computation.15 | async-start | bytes 1310720 | tf_op jit(solution)/shard_map/all_gather | solution.py:53
  196.0 147.0 %reduce-scatter.11.cloned.1.call-start = ((), (), s32[]{:S(2)}) async-start(), calls=%async_computation.19 | async-start | bytes 1310720 | tf_op jit(solution)/shard_map/reduce_scatter | solution.py:62
  235.4 27.5 %all-to-all-start.3 = ((bf16[32,12,1024]{2,1,0:T(8,128)(2,1)}), bf16[32,12,1024]{2,1,0:T(8,128)(2,1)S(1)}, u32[]{:S(2)}, u32[]{:S(2)}) async-start(bf16[32,12,1024]{2,1,0:T(8,128)(2,1)} %reshape.136), calls=%async_computation.4 | async-start | bytes 2097152 | tf_op jit(solution)/shard_map/all_to_all | solution.py:135
  264.4 30.9 %all-to-all-start.4 = ((bf16[32,32,128]{2,0,1:T(8,128)(2,1)}), bf16[32,32,128]{2,0,1:T(8,128)(2,1)S(1)}, u32[]{:S(2)}, u32[]{:S(2)}) async-start(bf16[32,32,128]{2,0,1:T(8,128)(2,1)} %copy.49), calls=%async_computation.5 | async-start | bytes 524288 | tf_op jit(solution)/shard_map/all_to_all | solution.py:149
  269.3 123.8 %reduce-scatter.9.cloned.1.call-start = ((), (), s32[]{:S(2)}) async-start(), calls=%async_computation.18 | async-start | bytes 1310720 | tf_op jit(solution)/shard_map/reduce_scatter | solution.py:159
  301.1 164.4 %reduce-scatter.7.cloned.1.call-start = ((), (), s32[]{:S(2)}) async-start(), calls=%async_computation.16 | async-start | bytes 8650752 | tf_op jit(solution)/shard_map/reduce_scatter | solution.py:153
  324.2 0.7 copy-start.6
  324.2 20.7 %copy-start.5 = (bf16[1,1024,1024]{2,1,0:T(8,128)(2,1)S(1)}, bf16[1,1024,1024]{2,1,0:T(8,128)(2,1)}, u32[]{:S(2)}) copy-start(bf16[1,1024,1024]{2,1,0:T(8,128)(2,1)} %param.16) | copy-start | bytes 6291460
  360.9 31.1 %all-to-all-start.6 = ((bf16[32,1,12]{2,1,0:T(2,128)(2,1)}), bf16[32,1,12]{2,1,0:T(2,128)(2,1)S(1)}, u32[]{:S(2)}, u32[]{:S(2)}) async-start(bf16[32,1,12]{2,1,0:T(2,128)(2,1)} %all_to_all.73), calls=%async_computation.10 | async-start | bytes 32768 | tf_op jit(solution)/shard_map/all_to_all | solution.py:136
  371.0 10.3 %copy-start.4 = (bf16[1,1536,1024]{2,1,0:T(8,128)(2,1)S(1)}, bf16[1,1536,1024]{2,1,0:T(8,128)(2,1)}, u32[]{:S(2)}) copy-start(bf16[1,1536,1024]{2,1,0:T(8,128)(2,1)} %all-gather.19.cloned.1.call-done) | copy-start | bytes 9437188
  371.0 10.3 %copy-start.8 = (bf16[1536,1024]{1,0:T(8,128)(2,1)S(1)}, bf16[1536,1024]{1,0:T(8,128)(2,1)}, u32[]{:S(2)}) copy-start(bf16[1536,1024]{1,0:T(8,128)(2,1)} %copy-done.7) | copy-start | bytes 9437188
  381.3 84.2 %copy-start.1 = (bf16[1,1024,1024]{2,1,0:T(8,128)(2,1)S(1)}, bf16[1,1024,1024]{2,1,0:T(8,128)(2,1)}, u32[]{:S(2)}) copy-start(bf16[1,1024,1024]{2,1,0:T(8,128)(2,1)} %param.15) | copy-start | bytes 6291460
Sparse Core Ops, SparseCore 0:
  9.7 26.4 all-gather.10
  38.5 54.4 all-gather.8
  94.7 38.9 all-gather.18
  140.7 37.3 all-gather.12
  194.8 38.4 reduce-scatter.4
  235.4 59.9 all-gather.16
  297.0 20.2 all-gather.14
  319.8 23.2 reduce-scatter.10
  345.6 23.8 reduce-scatter.8
  373.6 91.8 reduce-scatter.6
where the time goes:
time: 474 us; the launch traced here: 472 us
  waiting for transfers between devices  267 us (56%)
  matrix products  72.1 us (15%)
  blocking collectives  64.8 us (14%)
  starting transfers between devices  28.5 us (6%)
  local copies, waits for them, and re-layouts  21.6 us (5%)
  between operations  15.1 us (3%)
    reduce_scatter x1, waiting for transfers between devices, body(): lax.psum_scatter(contract_last(local, head_columns).astype(jnp.bfloat16),...  70.5 us
    all_gather x1, waiting for transfers between devices, body(): piece = lax.all_gather(out_grad, 'expert', axis=0, tiled=True)  56.8 us
    dot_general x4, matrix products, contract_last(): lax.dot_general(left, right, (((1,), (1,)), ((), ())), preferred_element_...  28.3 us
    dot_general x6, matrix products, contract_first(): lax.dot_general(left, right, (((0,), (0,)), ((), ())), preferred_element_...  27.4 us
    all_gather x1, waiting for transfers between devices, body(): lax.all_gather(layer_input, 'expert', axis=0, tiled=True)  25.8 us
    all_gather x1, waiting for transfers between devices, body(): merge_rows = lax.all_gather(merge_weight, 'group', axis=1, tiled=True)  24.9 us
    all_to_all x1, blocking collectives, body(): lax.all_to_all(outgoing, 'expert', split_axis=0, concat_axis=0, tiled=True)  20.9 us
    all_to_all x1, waiting for transfers between devices, body(): lax.all_to_all(back_rows, 'expert', split_axis=0, concat_axis=0, tiled=True)  19.8 us
  transfers between devices with their start and end apart: 14, of which 10 were waited for; matrix products, arithmetic and copies ran while one was open for 17% of the time, Pallas kernels for 0%

commit v1 on v0

v1 whole, which is shorter than its diff:
```python
import jax
import jax.numpy as jnp
from jax import lax
from jax.experimental import pallas as pl
from jax.experimental.pallas import tpu as pltpu
from jax.sharding import PartitionSpec as P

MESH = pl.DeviceIdType.MESH
BF = jnp.bfloat16
F32 = jnp.float32
MIB = 1 << 20

root_scale = 0.7978845608028654
cubic_term = 0.044715


def gelu_pair(value):
    square = value * value
    tangent = jnp.tanh(root_scale * value * (1.0 + cubic_term * square))
    half = 0.5 * (1.0 + tangent)
    slope = half + 0.5 * value * (1.0 - tangent * tangent) * root_scale * (
        1.0 + 3.0 * cubic_term * square
    )
    return value * half, slope


def dot(left, right, dims):
    return lax.dot_general(left, right, ((dims[:1], dims[1:]), ((), ())), preferred_element_type=F32)


NN, NT, TN = (1, 0), (1, 1), (0, 0)


def wrap(value):
    return lax.rem(value + 8, 4)


def place():
    e = lax.axis_index("expert")
    return lax.axis_index("group"), lax.rem(lax.div(e, 2), 4), lax.div(e, 8), lax.rem(e, 2)


def at(z, x, y, c):
    return {"group": z, "expert": (y * 4 + x) * 2 + c}


def by_chip(z, chip, c):
    return {"group": z, "expert": chip * 2 + c}


def rows(start, size):
    return pl.ds(pl.multiple_of(start, 16), size)


def lanes(start, size):
    return pl.ds(pl.multiple_of(start, 128), size)


def send(src, dst, ss, rs, device):
    pltpu.make_async_remote_copy(
        src_ref=src, dst_ref=dst, send_sem=ss, recv_sem=rs, device_id=device, device_id_type=MESH
    ).start()


def wait(ref, sem):
    pltpu.make_async_copy(ref, ref, sem).wait()


class PlaneGather:
    def __init__(self, buf, ss, rs, me):
        self.buf, self.ss, self.rs, self.me = buf, ss, rs, me
        self.sent = []

    def shift(self, h, i, j):
        z, x, y, c = self.me
        dx, dy = (i, j) if h == 0 else (j, i)
        return wrap(x + dx), wrap(y + dy)

    def piece(self, h, spot, half=None):
        px, py = self.shift(h, *spot)
        row = h * 512 + (py * 4 + px) * 32
        if half is None:
            return self.buf.at[rows(row, 32)]
        return self.buf.at[rows(row + 16 * half, 16)]

    def spot(self, stage, i, j):
        return (j, 0) if stage == 0 else (i, j)

    def sem(self, h, stage, i, kind):
        return h * 20 + (0 if stage == 0 else 4 + 4 * (i % 4)) + kind

    def go(self, ref, h, stage, i, kind, step):
        s = self.sem(h, stage, i, kind)
        px, py = self.shift(h, *((step, 0) if stage == 0 else (0, step)))
        send(ref, ref, self.ss.at[s], self.rs.at[s], at(self.me[0], px, py, self.me[3]))
        self.sent.append((ref, s))

    def begin(self, h, stage, i=0):
        ref = self.piece(h, self.spot(stage, i, 0))
        self.go(ref, h, stage, i, 0, 1)
        self.go(ref, h, stage, i, 1, -1)

    def take(self, h, stage, i, kind):
        spot = self.spot(stage, i, (-1, 1)[kind])
        wait(self.piece(h, spot), self.rs.at[self.sem(h, stage, i, kind)])
        self.go(self.piece(h, spot, kind), h, stage, i, kind + 2, (1, -1)[kind])

    def relay(self, h, stage, i=0):
        self.take(h, stage, i, 0)
        self.take(h, stage, i, 1)

    def finish(self, h, stage, i=0):
        for kind in (2, 3):
            ref = self.piece(h, self.spot(stage, i, 2), kind - 2)
            wait(ref, self.rs.at[self.sem(h, stage, i, kind)])

    def first(self, h):
        self.begin(h, 0)
        self.begin(h, 1, 0)

    def steps(self):
        for h in (0, 1):
            self.take(h, 0, 0, 0)
            self.begin(h, 1, -1)
            self.take(h, 0, 0, 1)
            self.begin(h, 1, 1)
        yield
        for h in (0, 1):
            self.relay(h, 1, 0)
        for h in (0, 1):
            self.finish(h, 0)
            self.begin(h, 1, 2)
        yield
        for i in (-1, 1):
            for h in (0, 1):
                self.relay(h, 1, i)
            yield
        for h in (0, 1):
            self.relay(h, 1, 2)
        yield
        for i in (0, -1, 1, 2):
            for h in (0, 1):
                self.finish(h, 1, i)
        yield
        for ref, s in self.sent:
            wait(ref, self.ss.at[s])


class PlaneScatter(PlaneGather):
    def __init__(self, buf, halves, wholes, ss, rs, me):
        super().__init__(buf, ss, rs, me)
        self.halves, self.wholes = halves, wholes

    def ring(self, h, stage, i):
        return h * 5 + (0 if stage == 0 else 1 + i % 4)

    def post(self, ref, dst, h, stage, i, kind, step):
        s = self.sem(h, stage, i, kind)
        px, py = self.shift(h, *((step, 0) if stage == 0 else (0, step)))
        send(ref, dst, self.ss.at[s], self.rs.at[s], at(self.me[0], px, py, self.me[3]))
        self.sent.append((ref, s))

    def open(self, h, stage, i=0):
        r = self.ring(h, stage, i)
        for kind, step in ((0, 1), (1, -1)):
            ref = self.piece(h, self.spot(stage, i, 2), kind)
            self.post(ref, self.halves.at[r, kind], h, stage, i, kind, step)

    def middle(self, h, stage, i=0):
        r = self.ring(h, stage, i)
        for kind, step in ((0, 1), (1, -1)):
            got = self.halves.at[r, kind]
            wait(got, self.rs.at[self.sem(h, stage, i, kind)])
            own = self.piece(h, self.spot(stage, i, step), kind)
            own[...] = (own[...].astype(F32) + got[...].astype(F32)).astype(BF)
            ref = self.piece(h, self.spot(stage, i, step))
            self.post(ref, self.wholes.at[r, kind], h, stage, i, kind + 2, step)

    def close(self, h, stage, i=0):
        r = self.ring(h, stage, i)
        for kind in (0, 1):
            wait(self.wholes.at[r, kind], self.rs.at[self.sem(h, stage, i, kind + 2)])
        own = self.piece(h, self.spot(stage, i, 0))
        own[...] = (
            own[...].astype(F32)
            + self.wholes[r, 0].astype(F32)
            + self.wholes[r, 1].astype(F32)
        ).astype(BF)

    def run(self):
        for i in (2, -1, 1, 0):
            for h in (0, 1):
                self.open(h, 1, i)
        for i in (2, -1, 1, 0):
            for h in (0, 1):
                self.middle(h, 1, i)
        for h in (0, 1):
            self.close(h, 1, 2)
            self.open(h, 0)
        for i in (-1, 1):
            for h in (0, 1):
                self.close(h, 1, i)
        for h in (0, 1):
            self.middle(h, 0)
        for h in (0, 1):
            self.close(h, 1, 0)
        for h in (0, 1):
            self.close(h, 0)

    def done(self):
        for ref, s in self.sent:
            wait(ref, self.ss.at[s])


class Fourfold:
    def __init__(self, src, slot, ss, rs, me):
        self.src, self.slot, self.ss, self.rs, self.me = src, slot, ss, rs, me
        z, x, y, c = me
        self.core = lax.div(z, 2)
        self.own = self.core == c

    def start(self):
        z, x, y, c = self.me
        dst = self.slot(lax.rem(z, 2), c)
        r = lax.rem(z, 2) * 2 + c

        @pl.when(self.own)
        def _():
            pltpu.make_async_copy(self.src, dst, self.rs.at[r]).start()

        @pl.when(jnp.logical_not(self.own))
        def _():
            send(self.src, dst, self.ss.at[0], self.rs.at[r], at(z, x, y, self.core))

        for k in (1, 3, 2):
            send(self.src, dst, self.ss.at[k], self.rs.at[r], at(wrap(z + k), x, y, self.core))

    def arrive(self):
        for i in (0, 1):
            for j in (0, 1):
                wait(self.slot(i, j), self.rs.at[i * 2 + j])

    def done(self):
        @pl.when(jnp.logical_not(self.own))
        def _():
            wait(self.src, self.ss.at[0])

        for k in (1, 2, 3):
            wait(self.src, self.ss.at[k])


class Fold:
    def __init__(self, out, got, ss, rs, me):
        self.out, self.got, self.ss, self.rs, self.me = out, got, ss, rs, me

    def start(self, i, j):
        z, x, y, c = self.me
        p = i * 2 + j
        to = 2 * c + i
        own = jnp.logical_and(to == z, c == j)

        @pl.when(own)
        def _():
            pltpu.make_async_copy(self.out.at[p], self.got.at[z], self.rs.at[z]).start()

        @pl.when(jnp.logical_not(own))
        def _():
            send(self.out.at[p], self.got.at[z], self.ss.at[p], self.rs.at[z], at(to, x, y, j))

    def arrive(self):
        for i in range(4):
            wait(self.got.at[i], self.rs.at[i])

    def done(self):
        z, x, y, c = self.me
        for i in (0, 1):
            for j in (0, 1):
                own = jnp.logical_and(2 * c + i == z, c == j)

                @pl.when(jnp.logical_not(own))
                def _():
                    wait(self.out.at[i * 2 + j], self.ss.at[i * 2 + j])


class ChipSwap:
    def __init__(self, src, dst, ss, rs, me):
        self.src, self.dst, self.ss, self.rs, self.me = src, dst, ss, rs, me
        self.chip = me[2] * 4 + me[1]

    def start(self):
        z, x, y, c = self.me
        mine = self.chip

        def step(k, _):
            to = lax.rem(mine + k, 16)
            send(self.src(to), self.dst(mine), self.ss.at[k], self.rs.at[k], by_chip(z, to, c))
            return 0

        pltpu.make_async_copy(self.src(mine), self.dst(mine), self.rs.at[0]).start()
        lax.fori_loop(1, 16, step, 0)

    def arrive(self):
        def step(k, _):
            wait(self.dst(lax.rem(self.chip + 16 - k, 16)), self.rs.at[k])
            return 0

        lax.fori_loop(0, 16, step, 0)

    def done(self):
        def step(k, _):
            wait(self.src(lax.rem(self.chip + k, 16)), self.ss.at[k])
            return 0

        lax.fori_loop(1, 16, step, 0)


class DeviceSwap:
    def __init__(self, out, got, ss, rs, z):
        self.out, self.got, self.ss, self.rs, self.z = out, got, ss, rs, z
        self.e = lax.axis_index("expert")

    def start(self):
        mine = self.e

        def step(k, _):
            to = lax.rem(mine + k, 32)
            send(
                self.out.at[rows(16 * to, 16)],
                self.got.at[rows(16 * mine, 16)],
                self.ss.at[k],
                self.rs.at[k],
                {"group": self.z, "expert": to},
            )
            return 0

        pltpu.make_async_copy(
            self.out.at[rows(16 * mine, 16)], self.got.at[rows(16 * mine, 16)], self.rs.at[0]
        ).start()
        lax.fori_loop(1, 32, step, 0)

    def arrive(self):
        def step(k, _):
            wait(self.got.at[rows(16 * lax.rem(self.e + 32 - k, 32), 16)], self.rs.at[k])
            return 0

        lax.fori_loop(0, 32, step, 0)

    def done(self):
        def step(k, _):
            wait(self.out.at[rows(16 * lax.rem(self.e + k, 32), 16)], self.ss.at[k])
            return 0

        lax.fori_loop(1, 32, step, 0)


class DepthGather:
    def __init__(self, src, buf, ss, rs, me):
        self.src, self.buf, self.ss, self.rs, self.me = src, buf, ss, rs, me

    def piece(self, step, half=None):
        row = 384 * wrap(self.me[0] + step)
        if half is None:
            return self.buf.at[rows(row, 384)]
        return self.buf.at[rows(row + 192 * half, 192)]

    def to(self, step):
        z, x, y, c = self.me
        return at(wrap(z + step), x, y, c)

    def start(self):
        dst = self.piece(0)
        send(self.src, dst, self.ss.at[0], self.rs.at[0], self.to(1))
        send(self.src, dst, self.ss.at[1], self.rs.at[1], self.to(-1))

    def take(self, kind):
        step = (-1, 1)[kind]
        wait(self.piece(step), self.rs.at[kind])
        half = self.piece(step, kind)
        send(half, half, self.ss.at[2 + kind], self.rs.at[2 + kind], self.to(-step))

    def finish(self, kind):
        wait(self.piece(2, kind), self.rs.at[2 + kind])

    def done(self):
        for kind in (0, 1):
            wait(self.src, self.ss.at[kind])
            wait(self.piece((-1, 1)[kind], kind), self.ss.at[2 + kind])


def dma(*shape):
    return pltpu.SemaphoreType.DMA(shape)


def merge_kernel(og, mw, merged, disp, tg, mgo, xin, buf, mwb, mc, sib_out, sib_in, tgc,
                 gs, gr, ws, wr, cs, cr, ts, tr, zs, zr, ls, bs, br):
    me = place()
    z, x, y, c = me
    chip = y * 4 + x
    other = at(z, x, y, 1 - c)
    mine = buf.at[rows(c * 512 + chip * 32, 32)]
    theirs = buf.at[rows((1 - c) * 512 + chip * 32, 32)]
    send(og.at[:, lanes((1 - c) * 2048, 2048)], mine, bs.at[0], br.at[0], other)
    local = pltpu.make_async_copy(og.at[:, lanes(c * 2048, 2048)], mine, ls.at[0])
    local.start()
    weights = Fourfold(
        mw, lambda i, j: mwb.at[rows(128 * j, 128), lanes(1024 * i, 1024)], ws, wr, me
    )
    weights.start()
    columns = ChipSwap(
        lambda to: merged.at[:, lanes(256 * to, 256)],
        lambda k: mc.at[rows(c * 512 + k * 32, 32)],
        cs, cr, me,
    )
    local.wait()
    wait(theirs, br.at[0])
    gather = PlaneGather(buf, gs, gr, me)
    for h in (0, 1):
        gather.first(h)
    columns.start()
    depth = DepthGather(disp, xin, zs, zr, me)
    depth.start()
    keep = pltpu.make_async_copy(disp, xin.at[rows(384 * z, 384)], ls.at[1])
    keep.start()
    for _ in gather.steps():
        pass
    weights.arrive()

    def product(h, tile):
        return dot(buf[rows(h * 512 + tile * 256, 256), :], mwb[...], NT)

    for tile in (0, 1):
        sib_out[pl.ds(tile * 256, 256), :] = product(1 - c, tile).astype(BF)
    send(sib_out, sib_in, bs.at[1], br.at[1], other)
    columns.arrive()
    half = mc.at[rows(c * 512, 512)]
    send(half, half, bs.at[2], br.at[2], other)
    own = [product(c, tile) for tile in (0, 1)]
    wait(sib_in, br.at[1])
    for tile in (0, 1):
        part = pl.ds(tile * 256, 256)
        tgc[part, :] = (own[tile] + sib_in[part, :].astype(F32)).astype(BF)
    tokens = ChipSwap(
        lambda to: tgc.at[rows(32 * to, 32)],
        lambda k: tg.at[:, lanes(256 * k, 256)],
        ts, tr, me,
    )
    tokens.start()
    depth.take(0)
    depth.take(1)
    wait(mc.at[rows((1 - c) * 512, 512)], br.at[2])
    for tile in range(4):
        sums = dot(mc[...], buf[:, tile * 512:tile * 512 + 512], TN).astype(BF)
        for j in (0, 1):
            mgo[(tile // 2) * 2 + j, :, (tile % 2) * 512:(tile % 2) * 512 + 512] = sums[
                128 * j:128 * j + 128
            ]
    tokens.arrive()
    depth.finish(0)
    depth.finish(1)
    keep.wait()
    weights.done()
    columns.done()
    tokens.done()
    depth.done()
    wait(mine, bs.at[0])
    wait(sib_out, bs.at[1])
    wait(half, bs.at[2])


def expert_kernel(tg, pg, sel, sums, mask, last, xin, w_in, w_out, li, hw,
                  hog, ing, outg, retg, lih, hwh,
                  outb, inb, sc, xv, wi, wo, hid, slope, bg, rp, fb, wb, sgo, sgi, back, ret,
                  s1, r1, s2, r2, gs, gr, hs, hr, zs, zr, fs, fr, qs, qr, ls, bs, br):
    me = place()
    z, x, y, c = me
    chip = y * 4 + x
    other = at(z, x, y, 1 - c)
    loads = [
        pltpu.make_async_copy(src, dst, ls.at[k])
        for k, (src, dst) in enumerate(((w_in, wi), (xin, xv), (w_out, wo)))
    ]
    for load in loads:
        load.start()
    for part in range(2):
        total = jnp.zeros((512, 512), F32)
        for h in range(4):
            first = h * 1024 + part * 512
            total = total + dot(pg[h], tg[:, first:first + 512], NN)
        outb[:, part * 512:part * 512 + 512] = total.astype(BF)
    there = DeviceSwap(outb, inb, s1, r1, z)
    there.start()
    head = Fourfold(
        hw, lambda i, j: hwh.at[rows(1024 * i, 1024), lanes(128 * j, 128)], hs, hr, me
    )
    head.start()
    mine = lih.at[rows(c * 512 + chip * 32, 32)]
    theirs = lih.at[rows((1 - c) * 512 + chip * 32, 32)]
    send(li.at[:, lanes((1 - c) * 2048, 2048)], mine, bs.at[0], br.at[0], other)
    keep = pltpu.make_async_copy(li.at[:, lanes(c * 2048, 2048)], mine, ls.at[3])
    keep.start()
    loads[0].wait()
    loads[1].wait()

    def early(t, _):
        part = rows(128 * t, 128)
        value, grade = gelu_pair(dot(xv[part, :], wi[...], NN))
        hid[part, :] = value.astype(BF)
        slope[part, :] = grade
        return 0

    lax.fori_loop(0, 12, early, 0)
    keep.wait()
    wait(theirs, br.at[0])
    there.arrive()
    own_rows = rows(384 * z, 384)
    sc[own_rows, :] = dot(sel[...], inb[...], NN).astype(BF)
    depth = DepthGather(sc.at[own_rows], sc, zs, zr, me)
    depth.start()
    gather = PlaneGather(lih, gs, gr, me)
    for h in (0, 1):
        gather.first(h)
    progress = gather.steps()
    loads[2].wait()

    def chunk(step):
        q = wrap(z + step)
        part = rows(384 * q, 384)
        grad = dot(sc[part, :], wo[...], NT)
        column = jnp.sum(grad * hid[part, :].astype(F32), axis=1, keepdims=True)
        sgo[q] = dot(sums[...], (column * mask[...]).astype(BF), NN).astype(BF)
        bg[part, :] = (grad * slope[part, :]).astype(BF)
        rp[part, :] = dot(bg[part, :], wi[...], NT).astype(BF)
        if step:
            send(sgo.at[q], sgi.at[z], qs.at[step], qr.at[4 - step], at(q, x, y, c))

    chunk(0)
    next(progress)
    depth.take(0)
    depth.take(1)
    next(progress)
    chunk(1)
    chunk(3)
    next(progress)
    depth.finish(0)
    depth.finish(1)
    chunk(2)

    def rowpart(step, half=None):
        row = 384 * wrap(z + step)
        if half is None:
            return rp.at[rows(row, 384)]
        return rp.at[rows(row + 192 * half, 192)]

    for kind, step in ((0, 1), (1, -1)):
        send(rowpart(2, kind), fb.at[kind], fs.at[kind], fr.at[kind], at(wrap(z + step), x, y, c))
    next(progress)
    for kind, step in ((0, 1), (1, -1)):
        wait(fb.at[kind], fr.at[kind])
        target = rowpart(step, kind)
        target[...] = (target[...].astype(F32) + fb[kind].astype(F32)).astype(BF)
        send(rowpart(step), wb.at[kind], fs.at[2 + kind], fr.at[2 + kind],
             at(wrap(z + step), x, y, c))
    next(progress)

    def weight(t, _):
        part = lanes(256 * t, 256)
        ing[:, part] = dot(xv[...], bg[:, part], TN)
        outg[:, part] = dot(hid[...], sc[:, part], TN)
        return 0

    lax.fori_loop(0, 4, weight, 0)
    for step in (1, 2, 3):
        wait(sgi.at[wrap(z + step)], qr.at[step])
    marks = sgo[z].astype(F32)
    for step in (1, 2, 3):
        marks = marks + sgi[wrap(z + step)].astype(F32)
    for kind in (0, 1):
        wait(wb.at[kind], fr.at[2 + kind])
    total = (rp[own_rows, :].astype(F32) + wb[0].astype(F32) + wb[1].astype(F32)).astype(BF)
    back[...] = dot(sel[...], total, TN).astype(BF)
    spread = dot(last[...], marks.astype(BF), NN)
    back[:, 0:128] = (back[:, 0:128].astype(F32) + spread).astype(BF)
    home = DeviceSwap(back, ret, s2, r2, z)
    home.start()
    for _ in progress:
        pass
    head.arrive()
    home.arrive()
    for h in range(4):
        hog[:, h * 1024:h * 1024 + 1024] = dot(pg[h], ret[...], TN).astype(BF)
    retg[...] = ret[:, 0:128]
    there.done()
    home.done()
    head.done()
    depth.done()
    wait(mine, bs.at[0])
    for step in (1, 2, 3):
        wait(sgo.at[wrap(z + step)], qs.at[step])
    for kind in (0, 1):
        wait(rowpart(2, kind), fs.at[kind])
        wait(rowpart((1, -1)[kind]), fs.at[2 + kind])


def head_kernel(hog, lih, hwh, mgo, ig, hg, mg,
                hc, part, liv, hwv, halves, wholes, hgo, hgi, mgi,
                cs, cr, gs, gr, hs, hr, ms, mr, ls, bs, br):
    me = place()
    z, x, y, c = me
    chip = y * 4 + x
    other = at(z, x, y, 1 - c)
    columns = ChipSwap(
        lambda to: hog.at[:, lanes(256 * to, 256)],
        lambda k: hc.at[rows(c * 512 + k * 32, 32)],
        cs, cr, me,
    )
    columns.start()
    loads = [
        pltpu.make_async_copy(src, dst, ls.at[k])
        for k, (src, dst) in enumerate(((hwh, hwv), (lih, liv)))
    ]
    for load in loads:
        load.start()
    merge = Fold(mgo, mgi, ms, mr, me)
    for i in (0, 1):
        for j in (0, 1):
            merge.start(i, j)
    columns.arrive()
    half = hc.at[rows(c * 512, 512)]
    send(half, half, bs.at[0], br.at[0], other)
    loads[0].wait()

    def product(h):
        def step(t, _):
            tile = rows(h * 512 + 128 * t, 128)
            part[tile, :] = dot(hc[tile, :], hwv[...], NT).astype(BF)
            return 0

        lax.fori_loop(0, 4, step, 0)

    product(c)
    wait(hc.at[rows((1 - c) * 512, 512)], br.at[0])
    product(1 - c)
    scatter = PlaneScatter(part, halves, wholes, gs, gr, me)
    loads[1].wait()
    head = Fold(hgo, hgi, hs, hr, me)
    scatter.run()
    for i in (0, 1):
        for tile in (0, 1):
            sums = dot(liv[:, i * 1024 + tile * 512:i * 1024 + tile * 512 + 512], hc[...], TN)
            for j in (0, 1):
                hgo[i * 2 + j, tile * 512:tile * 512 + 512, :] = sums[
                    :, 128 * j:128 * j + 128
                ].astype(BF)
        for j in (0, 1):
            head.start(i, j)
    give = part.at[rows((1 - c) * 512 + chip * 32, 32)]
    mine = part.at[rows(c * 512 + chip * 32, 32)]
    seen = ig.at[:, lanes((1 - c) * 2048, 2048)]
    there = ig.at[:, lanes(c * 2048, 2048)]
    send(give, there, bs.at[1], br.at[1], other)
    keep = pltpu.make_async_copy(mine, there, ls.at[2])
    keep.start()
    merge.arrive()
    mg[...] = (mgi[0].astype(F32) + mgi[1].astype(F32)) + (mgi[2].astype(F32) + mgi[3].astype(F32))
    head.arrive()
    hg[...] = (hgi[0].astype(F32) + hgi[1].astype(F32)) + (hgi[2].astype(F32) + hgi[3].astype(F32))
    wait(seen, br.at[1])
    keep.wait()
    scatter.done()
    columns.done()
    merge.done()
    head.done()
    wait(half, bs.at[0])
    wait(give, bs.at[1])


VM = pl.BlockSpec(memory_space=pltpu.VMEM)
ANY = pl.BlockSpec(memory_space=pl.ANY)


def call(kernel, operands, specs, outs, out_specs, scratch, limit, flops):
    return pl.pallas_call(
        kernel,
        out_shape=[jax.ShapeDtypeStruct(shape, kind) for shape, kind in outs],
        in_specs=specs,
        out_specs=out_specs,
        scratch_shapes=[pltpu.VMEM(s[0], s[1]) if isinstance(s, tuple) else s for s in scratch],
        compiler_params=pltpu.CompilerParams(
            has_side_effects=True, vmem_limit_bytes=limit * MIB
        ),
        cost_estimate=pl.CostEstimate(flops=flops, bytes_accessed=1 << 24, transcendentals=0),
    )(*operands)


def body(
    layer_input, out_grad, merged, head_weight, merge_weight,
    expert_in, expert_out, dispatched, expert_ids, gate_values,
):
    flat_ids = expert_ids.reshape(-1)
    onehot = (flat_ids[:, None] == jnp.arange(32, dtype=jnp.int32)[None, :]).astype(jnp.int32)
    ranks = jnp.sum(onehot * jnp.cumsum(onehot, axis=0), axis=1) - 1
    targets = (flat_ids * 16 + ranks).reshape(32, 4, 2).transpose(1, 0, 2)
    gates = gate_values.astype(F32).reshape(32, 4, 2).transpose(1, 0, 2)
    slots = jnp.arange(512, dtype=jnp.int32)[None, :, None]
    pg = (
        jnp.where(slots == targets[:, None, :, 0], gates[:, None, :, 0], 0.0)
        + jnp.where(slots == targets[:, None, :, 1], gates[:, None, :, 1], 0.0)
    ).astype(BF)
    row = jnp.arange(384, dtype=jnp.int32)[:, None]
    sel = ((row // 12) * 16 + row % 12 == jnp.arange(512, dtype=jnp.int32)[None, :]).astype(BF)
    sums = (jnp.arange(32, dtype=jnp.int32)[:, None] == (row // 12).reshape(1, 384)).astype(BF)
    mask = (row % 12 == jnp.arange(128, dtype=jnp.int32)[None, :]).astype(F32)
    last = (
        jnp.arange(512, dtype=jnp.int32)[:, None]
        == jnp.arange(32, dtype=jnp.int32)[None, :] * 16 + 12
    ).astype(BF)

    tg, mgo, xin = call(
        merge_kernel,
        (out_grad, merge_weight, merged, dispatched[0]),
        [ANY] * 4,
        [((32, 4096), BF), ((4, 128, 1024), BF), ((1536, 1024), BF)],
        [VM, VM, ANY],
        [
            ((1024, 2048), BF), ((256, 2048), BF), ((1024, 256), BF),
            ((512, 256), BF), ((512, 256), BF), ((512, 256), BF),
            dma(40), dma(40), dma(4), dma(4), dma(16), dma(16), dma(16), dma(16),
            dma(4), dma(4), dma(2), dma(3), dma(3),
        ],
        32, 1 << 31,
    )
    hog, in_grad, out_weight_grad, retg, lih, hwh = call(
        expert_kernel,
        (tg, pg, sel, sums, mask, last, xin, expert_in[0], expert_out[0], layer_input, head_weight),
        [VM] * 6 + [ANY] * 5,
        [
            ((32, 4096), BF), ((1024, 1024), F32), ((1024, 1024), F32), ((512, 128), BF),
            ((1024, 2048), BF), ((2048, 256), BF),
        ],
        [VM, VM, VM, VM, ANY, ANY],
        [
            ((512, 1024), BF), ((512, 1024), BF), ((1536, 1024), BF), ((1536, 1024), BF),
            ((1024, 1024), BF), ((1024, 1024), BF), ((1536, 1024), BF), ((1536, 1024), F32),
            ((1536, 1024), BF), ((1536, 1024), BF), ((2, 192, 1024), BF), ((2, 384, 1024), BF),
            ((4, 32, 128), BF), ((4, 32, 128), BF), ((512, 1024), BF), ((512, 1024), BF),
            dma(32), dma(32), dma(32), dma(32), dma(40), dma(40), dma(4), dma(4),
            dma(4), dma(4), dma(4), dma(4), dma(4), dma(4), dma(4), dma(1), dma(1),
        ],
        56, 1 << 34,
    )
    input_total, head_grad, merge_grad = call(
        head_kernel,
        (hog, lih, hwh, mgo),
        [VM, ANY, ANY, VM],
        [((32, 4096), BF), ((1024, 128), F32), ((128, 1024), F32)],
        [VM, VM, VM],
        [
            ((1024, 256), BF), ((1024, 2048), BF), ((1024, 2048), BF), ((2048, 256), BF),
            ((10, 2, 16, 2048), BF), ((10, 2, 32, 2048), BF),
            ((4, 1024, 128), BF), ((4, 1024, 128), BF), ((4, 128, 1024), BF),
            dma(16), dma(16), dma(40), dma(40), dma(4), dma(4), dma(4), dma(4),
            dma(3), dma(2), dma(2),
        ],
        40, 1 << 31,
    )
    found = jnp.dot(
        onehot.astype(BF), retg.reshape(32, 16, 128)[:, 12, :], preferred_element_type=F32
    )
    spot = ranks[:, None] == jnp.arange(128, dtype=jnp.int32)[None, :]
    gate_grad = (
        jnp.sum(jnp.where(spot, found, 0.0), axis=1).reshape(128, 2) / gate_values.astype(F32)
    ).astype(BF)
    return (input_total, head_grad, merge_grad, in_grad[None], out_weight_grad[None], gate_grad)


def solution(mesh):
    placed = (
        P(("group", "expert"), None),
        P(("group", "expert"), None),
        P(("group", "expert"), None),
        P("group", "expert"),
        P("expert", "group"),
        P("expert", None, "group"),
        P("expert", "group", None),
        P("expert", "group", None),
        P(("group", "expert"), None),
        P(("group", "expert"), None),
    )
    return jax.shard_map(
        body,
        mesh=mesh,
        in_specs=placed,
        out_specs=(
            P(("group", "expert"), None),
            P("group", "expert"),
            P("expert", "group"),
            P("expert", None, "group"),
            P("expert", "group", None),
            P(("group", "expert"), None),
        ),
        check_vma=False,
    )
```

time: 474 us -> 257 us (0.54)
  waiting for transfers between devices: 267 us -> 0 us
  Pallas kernels: 0 us -> 226 us
  matrix products: 72.1 us -> 0.23 us
  blocking collectives: 64.8 us -> 0 us
  starting transfers between devices: 28.5 us -> 0 us
  between operations: 15.1 us -> 0.78 us
    pallas_call x0 -> x3, Pallas kernels: none -> 226 us  [call(): pl.pallas_call(kernel, out_shape=[jax.ShapeDtypeStruct(shape, kind) for s...]
    all_gather x6 -> x0, waiting for transfers between devices: 133 us -> none  [the longest x1 56.8 us: body(): piece = lax.all_gather(out_grad, 'expert', axis=0, tiled=True)]
    reduce_scatter x4 -> x0, waiting for transfers between devices: 103 us -> none  [the longest x1 70.5 us: body(): lax.psum_scatter(contract_last(local, head_columns).astype(jnp.bfloat16),...]
    dot_general x14 -> x1, matrix products: 72.1 us -> 0.23 us  [body(): jnp.dot(onehot.astype(BF), retg.reshape(32, 16, 128)[:, 12, :], preferred...]
    all_to_all x3 -> x0, blocking collectives: 47.5 us -> none  [the longest x1 20.9 us: body(): lax.all_to_all(outgoing, 'expert', split_axis=0, concat_axis=0, tiled=True)]
    all_to_all x4 -> x0, waiting for transfers between devices: 28.5 us -> none  [the longest x1 19.8 us: body(): lax.all_to_all(back_rows, 'expert', split_axis=0, concat_axis=0, tiled=True)]
    all_to_all x4 -> x0, starting transfers between devices: 27.9 us -> none  [the longest x1 10.1 us: body(): lax.all_to_all(back_gates, 'expert', split_axis=0, concat_axis=0, tiled=T...]
    unnamed x26 -> x28, local copies, waits for them, and re-layouts: 12.1 us -> 22.1 us
  transfers between devices with their start and end apart: 14 -> 0, of which waited for: 10 -> 0; matrix products, arithmetic and copies ran while one was open for 17% -> 0% of each run, Pallas kernels for 0% -> 0%
where the time goes in v1:
time: 257 us
  Pallas kernels  226 us (88%)
  local copies, waits for them, and re-layouts  24.8 us (10%)
  other arithmetic  5.47 us (2%)
    pallas_call x3, Pallas kernels, call(): pl.pallas_call(kernel, out_shape=[jax.ShapeDtypeStruct(shape, kind) for s...  226 us
    unnamed x28, local copies, waits for them, and re-layouts  22.1 us

profile of v1, /device:TPU:1, one launch (start us, length us, event | category | flops | bytes accessed | tf_op | source)
XLA Modules:
  0.0 257.0 jit_solution(5147682636195207182)
XLA Ops:
  2.1 0.8 copy.23
  3.4 0.8 copy.18
  6.1 0.7 fusion.2.last
  6.8 0.8 fusion.3.mask
  7.5 0.9 fusion.1.sel
  8.4 1.0 add_convert_fusion.pg
  9.4 1.1 copy-done
  10.6 0.9 copy-done.1
  11.5 0.9 copy-done.2
  12.5 0.9 copy-done.3
  13.4 58.6 %shard_map.145 = (bf16[32,4096]{1,0:T(8,128)(2,1)S(1)}, bf16[4,128,1024]{2,1,0:T(8,128)(2,1)S(1)}, bf16[1536,1024]{1,0:T(8,128)(2,1)S(1)}) custom-call(bf16[32,4096]{1,0:T(8,128)(2,1)S(1)} %copy-done.1, bf16[128,1024]{1,0:T(8,128)(2,1)S(1)} %copy-done.2, bf16[32,4096]{1,0:T(8,128)(2,1)S(1)} %copy-done.3, bf16[384,1024]{1,0:T(8,128)(2,1)S(1)} %bitcast.35), custom_call_target="tpu_custom_call" | custom-call | flops 2147483648 | bytes 16777216 | tf_op jit(solution)/shard_map/pallas_call | solution.py:682
  72.1 1.7 copy-done.7
  73.7 0.7 copy-done.8
  74.4 106.9 %shard_map.146 = (bf16[32,4096]{1,0:T(8,128)(2,1)}, f32[1024,1024]{1,0:T(8,128)}, f32[1024,1024]{1,0:T(8,128)}, bf16[512,128]{1,0:T(8,128)(2,1)}, bf16[1024,2048]{1,0:T(8,128)(2,1)}, /*index=5*/bf16[2048,256]{1,0:T(8,128)(2,1)}) custom-call(bf16[32,4096]{1,0:T(8,128)(2,1)} %copy-done.8, bf16[4,512,32]{2,1,0:T(8,128)(2,1)} %add_convert_fusion.pg, ...), custom_call_target="tpu_custom_call" | custom-call | flops 17179869184 | bytes 16777216 | tf_op jit(solution)/shard_map/pallas_call | solution.py:682
  181.3 2.2 copy-done.4
  183.5 1.2 copy-done.5
  184.8 0.9 copy-done.6
  185.7 60.2 %shard_map.147 = (bf16[32,4096]{1,0:T(8,128)(2,1)S(1)}, f32[1024,128]{1,0:T(8,128)S(1)}, f32[128,1024]{1,0:T(8,128)S(1)}) custom-call(bf16[32,4096]{1,0:T(8,128)(2,1)S(1)} %copy-done.6, bf16[1024,2048]{1,0:T(8,128)(2,1)S(1)} %copy-done.4, bf16[2048,256]{1,0:T(8,128)(2,1)S(1)} %copy-done.5, bf16[4,128,1024]{2,1,0:T(8,128)(2,1)S(1)} %get-tuple-element.23.mgo), custom_call_target="tpu_custom_call" | custom-call | flops 2147483648 | bytes 16777216 | tf_op jit(solution)/shard_map/pallas_call | solution.py:682
  245.9 0.9 slice.33
  247.8 0.7 copy.41
  248.5 0.8 copy.42
  249.3 0.8 copy.43
  250.1 4.9 %copy.44 = f32[1,1024,1024]{2,1,0:T(8,128)} copy(f32[1,1024,1024]{2,1,0:T(8,128)} %bitcast.37) | data formatting | bytes 8388608
  255.0 2.0 copy.45
  (41 shorter events, 4.8 us)
Async XLA Ops:
  9.4 1.1 copy-start
  10.6 0.9 copy-start.1
  11.5 0.9 copy-start.2
  12.5 0.9 copy-start.3
  72.1 1.7 copy-start.7
  73.7 0.7 copy-start.8
  181.3 2.2 copy-start.4
  183.5 1.2 copy-start.5
  184.8 0.9 copy-start.6
  250.1 4.9 %copy-start.9 = (f32[1024,1024]{1,0:T(8,128)S(1)}, f32[1024,1024]{1,0:T(8,128)}, u32[]{:S(2)}) copy-start(f32[1024,1024]{1,0:T(8,128)} %get-tuple-element.28) | copy-start | bytes 12582916

commit v2 on v1

v2 whole, which is shorter than its diff:
```python
import jax
import jax.numpy as jnp
from jax import lax
from jax.experimental import pallas as pl
from jax.experimental.pallas import tpu as pltpu
from jax.sharding import PartitionSpec as P

MESH = pl.DeviceIdType.MESH
BF = jnp.bfloat16
F32 = jnp.float32
LIMIT = 63 << 20

root_scale = 0.7978845608028654
cubic_term = 0.044715


def gelu_pair(value):
    square = value * value
    tangent = jnp.tanh(root_scale * value * (1.0 + cubic_term * square))
    half = 0.5 * (1.0 + tangent)
    slope = half + 0.5 * value * (1.0 - tangent * tangent) * root_scale * (
        1.0 + 3.0 * cubic_term * square
    )
    return value * half, slope


def dot(left, right, dims):
    return lax.dot_general(left, right, ((dims[:1], dims[1:]), ((), ())), preferred_element_type=F32)


NN, NT, TN = (1, 0), (1, 1), (0, 0)


def wrap(value):
    return lax.rem(value + 8, 4)


def place():
    e = lax.axis_index("expert")
    return lax.axis_index("group"), lax.rem(lax.div(e, 2), 4), lax.div(e, 8), lax.rem(e, 2)


def at(z, x, y, c):
    return {"group": z, "expert": (y * 4 + x) * 2 + c}


def by_chip(z, chip, c):
    return {"group": z, "expert": chip * 2 + c}


def rows(start, size):
    return pl.ds(pl.multiple_of(start, 16), size)


def lanes(start, size):
    return pl.ds(pl.multiple_of(start, 128), size)


def send(src, dst, ss, rs, device):
    pltpu.make_async_remote_copy(
        src_ref=src, dst_ref=dst, send_sem=ss, recv_sem=rs, device_id=device, device_id_type=MESH
    ).start()


def wait(ref, sem):
    pltpu.make_async_copy(ref, ref, sem).wait()


class PlaneGather:
    def __init__(self, buf, ss, rs, me):
        self.buf, self.ss, self.rs, self.me = buf, ss, rs, me
        self.sent = []

    def shift(self, h, i, j):
        z, x, y, c = self.me
        dx, dy = (i, j) if h == 0 else (j, i)
        return wrap(x + dx), wrap(y + dy)

    def piece(self, h, spot, half=None):
        px, py = self.shift(h, *spot)
        row = h * 512 + (py * 4 + px) * 32
        if half is None:
            return self.buf.at[rows(row, 32)]
        return self.buf.at[rows(row + 16 * half, 16)]

    def spot(self, stage, i, j):
        return (j, 0) if stage == 0 else (i, j)

    def sem(self, h, stage, i, kind):
        return h * 20 + (0 if stage == 0 else 4 + 4 * (i % 4)) + kind

    def go(self, ref, h, stage, i, kind, step):
        s = self.sem(h, stage, i, kind)
        px, py = self.shift(h, *((step, 0) if stage == 0 else (0, step)))
        send(ref, ref, self.ss.at[s], self.rs.at[s], at(self.me[0], px, py, self.me[3]))
        self.sent.append((ref, s))

    def begin(self, h, stage, i=0):
        ref = self.piece(h, self.spot(stage, i, 0))
        self.go(ref, h, stage, i, 0, 1)
        self.go(ref, h, stage, i, 1, -1)

    def take(self, h, stage, i, kind):
        spot = self.spot(stage, i, (-1, 1)[kind])
        wait(self.piece(h, spot), self.rs.at[self.sem(h, stage, i, kind)])
        self.go(self.piece(h, spot, kind), h, stage, i, kind + 2, (1, -1)[kind])

    def relay(self, h, stage, i=0):
        self.take(h, stage, i, 0)
        self.take(h, stage, i, 1)

    def finish(self, h, stage, i=0):
        for kind in (2, 3):
            ref = self.piece(h, self.spot(stage, i, 2), kind - 2)
            wait(ref, self.rs.at[self.sem(h, stage, i, kind)])

    def first(self, h):
        self.begin(h, 0)
        self.begin(h, 1, 0)

    def steps(self):
        for h in (0, 1):
            self.take(h, 0, 0, 0)
            self.begin(h, 1, -1)
            self.take(h, 0, 0, 1)
            self.begin(h, 1, 1)
        yield
        for h in (0, 1):
            self.relay(h, 1, 0)
        for h in (0, 1):
            self.finish(h, 0)
            self.begin(h, 1, 2)
        yield
        for i in (-1, 1):
            for h in (0, 1):
                self.relay(h, 1, i)
            yield
        for h in (0, 1):
            self.relay(h, 1, 2)
        yield
        for i in (0, -1, 1, 2):
            for h in (0, 1):
                self.finish(h, 1, i)
        yield
        for ref, s in self.sent:
            wait(ref, self.ss.at[s])


class PlaneScatter(PlaneGather):
    def __init__(self, buf, halves, wholes, ss, rs, me):
        super().__init__(buf, ss, rs, me)
        self.halves, self.wholes = halves, wholes

    def ring(self, h, stage, i):
        return h * 5 + (0 if stage == 0 else 1 + i % 4)

    def post(self, ref, dst, h, stage, i, kind, step):
        s = self.sem(h, stage, i, kind)
        px, py = self.shift(h, *((step, 0) if stage == 0 else (0, step)))
        send(ref, dst, self.ss.at[s], self.rs.at[s], at(self.me[0], px, py, self.me[3]))
        self.sent.append((ref, s))

    def open(self, h, stage, i=0):
        r = self.ring(h, stage, i)
        for kind, step in ((0, 1), (1, -1)):
            ref = self.piece(h, self.spot(stage, i, 2), kind)
            self.post(ref, self.halves.at[r, kind], h, stage, i, kind, step)

    def middle(self, h, stage, i=0):
        r = self.ring(h, stage, i)
        for kind, step in ((0, 1), (1, -1)):
            got = self.halves.at[r, kind]
            wait(got, self.rs.at[self.sem(h, stage, i, kind)])
            own = self.piece(h, self.spot(stage, i, step), kind)
            own[...] = (own[...].astype(F32) + got[...].astype(F32)).astype(BF)
            ref = self.piece(h, self.spot(stage, i, step))
            self.post(ref, self.wholes.at[r, kind], h, stage, i, kind + 2, step)

    def close(self, h, stage, i=0):
        r = self.ring(h, stage, i)
        for kind in (0, 1):
            wait(self.wholes.at[r, kind], self.rs.at[self.sem(h, stage, i, kind + 2)])
        own = self.piece(h, self.spot(stage, i, 0))
        own[...] = (
            own[...].astype(F32)
            + self.wholes[r, 0].astype(F32)
            + self.wholes[r, 1].astype(F32)
        ).astype(BF)

    def begin_all(self):
        for i in (2, -1, 1, 0):
            for h in (0, 1):
                self.open(h, 1, i)

    def run(self):
        for i in (2, -1, 1, 0):
            for h in (0, 1):
                self.middle(h, 1, i)
        for h in (0, 1):
            self.close(h, 1, 2)
            self.open(h, 0)
        for i in (-1, 1):
            for h in (0, 1):
                self.close(h, 1, i)
        for h in (0, 1):
            self.middle(h, 0)
        for h in (0, 1):
            self.close(h, 1, 0)
        for h in (0, 1):
            self.close(h, 0)

    def done(self):
        for ref, s in self.sent:
            wait(ref, self.ss.at[s])


class Fourfold:
    def __init__(self, src, slot, ss, rs, me):
        self.src, self.slot, self.ss, self.rs, self.me = src, slot, ss, rs, me
        z, x, y, c = me
        self.core = lax.div(z, 2)
        self.own = self.core == c

    def start(self):
        z, x, y, c = self.me
        dst = self.slot(lax.rem(z, 2), c)
        r = lax.rem(z, 2) * 2 + c

        @pl.when(self.own)
        def _():
            pltpu.make_async_copy(self.src, dst, self.rs.at[r]).start()

        @pl.when(jnp.logical_not(self.own))
        def _():
            send(self.src, dst, self.ss.at[0], self.rs.at[r], at(z, x, y, self.core))

        for k in (1, 3, 2):
            send(self.src, dst, self.ss.at[k], self.rs.at[r], at(wrap(z + k), x, y, self.core))

    def arrive(self):
        for i in (0, 1):
            for j in (0, 1):
                wait(self.slot(i, j), self.rs.at[i * 2 + j])

    def done(self):
        @pl.when(jnp.logical_not(self.own))
        def _():
            wait(self.src, self.ss.at[0])

        for k in (1, 2, 3):
            wait(self.src, self.ss.at[k])


class Fold:
    def __init__(self, out, got, ss, rs, me):
        self.out, self.got, self.ss, self.rs, self.me = out, got, ss, rs, me

    def start(self, i, j):
        z, x, y, c = self.me
        p = i * 2 + j
        to = 2 * c + i
        own = jnp.logical_and(to == z, c == j)

        @pl.when(own)
        def _():
            pltpu.make_async_copy(self.out.at[p], self.got.at[z], self.rs.at[z]).start()

        @pl.when(jnp.logical_not(own))
        def _():
            send(self.out.at[p], self.got.at[z], self.ss.at[p], self.rs.at[z], at(to, x, y, j))

    def arrive(self):
        for i in range(4):
            wait(self.got.at[i], self.rs.at[i])

    def done(self):
        z, x, y, c = self.me
        for i in (0, 1):
            for j in (0, 1):
                own = jnp.logical_and(2 * c + i == z, c == j)

                @pl.when(jnp.logical_not(own))
                def _():
                    wait(self.out.at[i * 2 + j], self.ss.at[i * 2 + j])


class ChipSwap:
    def __init__(self, src, dst, ss, rs, me):
        self.src, self.dst, self.ss, self.rs, self.me = src, dst, ss, rs, me
        self.chip = me[2] * 4 + me[1]

    def start(self):
        z, x, y, c = self.me
        mine = self.chip

        def step(k, _):
            to = lax.rem(mine + k, 16)
            send(self.src(to), self.dst(mine), self.ss.at[k], self.rs.at[k], by_chip(z, to, c))
            return 0

        pltpu.make_async_copy(self.src(mine), self.dst(mine), self.rs.at[0]).start()
        lax.fori_loop(1, 16, step, 0)

    def arrive(self):
        def step(k, _):
            wait(self.dst(lax.rem(self.chip + 16 - k, 16)), self.rs.at[k])
            return 0

        lax.fori_loop(0, 16, step, 0)

    def done(self):
        def step(k, _):
            wait(self.src(lax.rem(self.chip + k, 16)), self.ss.at[k])
            return 0

        lax.fori_loop(1, 16, step, 0)


class DeviceSwap:
    def __init__(self, out, got, ss, rs, z):
        self.out, self.got, self.ss, self.rs, self.z = out, got, ss, rs, z
        self.e = lax.axis_index("expert")

    def start(self):
        mine = self.e

        def step(k, _):
            to = lax.rem(mine + k, 32)
            send(
                self.out.at[rows(16 * to, 16)],
                self.got.at[rows(16 * mine, 16)],
                self.ss.at[k],
                self.rs.at[k],
                {"group": self.z, "expert": to},
            )
            return 0

        pltpu.make_async_copy(
            self.out.at[rows(16 * mine, 16)], self.got.at[rows(16 * mine, 16)], self.rs.at[0]
        ).start()
        lax.fori_loop(1, 32, step, 0)

    def arrive(self):
        def step(k, _):
            wait(self.got.at[rows(16 * lax.rem(self.e + 32 - k, 32), 16)], self.rs.at[k])
            return 0

        lax.fori_loop(0, 32, step, 0)

    def done(self):
        def step(k, _):
            wait(self.out.at[rows(16 * lax.rem(self.e + k, 32), 16)], self.ss.at[k])
            return 0

        lax.fori_loop(1, 32, step, 0)


class DepthGather:
    def __init__(self, buf, cols, ss, rs, me):
        self.buf, self.cols, self.ss, self.rs, self.me = buf, cols, ss, rs, me

    def piece(self, step, half=None):
        row = 384 * wrap(self.me[0] + step)
        if half is None:
            return self.buf.at[rows(row, 384), self.cols]
        return self.buf.at[rows(row + 192 * half, 192), self.cols]

    def to(self, step):
        z, x, y, c = self.me
        return at(wrap(z + step), x, y, c)

    def start(self):
        own = self.piece(0)
        send(own, own, self.ss.at[0], self.rs.at[0], self.to(1))
        send(own, own, self.ss.at[1], self.rs.at[1], self.to(-1))

    def take(self, kind):
        step = (-1, 1)[kind]
        wait(self.piece(step), self.rs.at[kind])
        half = self.piece(step, kind)
        send(half, half, self.ss.at[2 + kind], self.rs.at[2 + kind], self.to(-step))

    def finish(self):
        for kind in (0, 1):
            wait(self.piece(2, kind), self.rs.at[2 + kind])

    def done(self):
        for kind in (0, 1):
            wait(self.piece(0), self.ss.at[kind])
            wait(self.piece((-1, 1)[kind], kind), self.ss.at[2 + kind])


class DepthScatter:
    def __init__(self, buf, cols, halves, wholes, ss, rs, me):
        self.buf, self.cols, self.halves, self.wholes = buf, cols, halves, wholes
        self.ss, self.rs, self.me = ss, rs, me

    def piece(self, step, half=None):
        row = 384 * wrap(self.me[0] + step)
        if half is None:
            return self.buf.at[rows(row, 384), self.cols]
        return self.buf.at[rows(row + 192 * half, 192), self.cols]

    def to(self, step):
        z, x, y, c = self.me
        return at(wrap(z + step), x, y, c)

    def open(self):
        for kind, step in ((0, 1), (1, -1)):
            send(self.piece(2, kind), self.halves.at[kind], self.ss.at[kind], self.rs.at[kind],
                 self.to(step))

    def middle(self):
        for kind, step in ((0, 1), (1, -1)):
            wait(self.halves.at[kind], self.rs.at[kind])
            own = self.piece(step, kind)
            own[...] = (own[...].astype(F32) + self.halves[kind].astype(F32)).astype(BF)
            send(self.piece(step), self.wholes.at[kind], self.ss.at[2 + kind],
                 self.rs.at[2 + kind], self.to(step))

    def close(self):
        for kind in (0, 1):
            wait(self.wholes.at[kind], self.rs.at[2 + kind])
        return (
            self.piece(0)[...].astype(F32)
            + self.wholes[0].astype(F32)
            + self.wholes[1].astype(F32)
        ).astype(BF)

    def done(self):
        for kind, step in ((0, 1), (1, -1)):
            wait(self.piece(2, kind), self.ss.at[kind])
            wait(self.piece(step), self.ss.at[2 + kind])


def dma(*shape):
    return pltpu.SemaphoreType.DMA(shape)


def iota(shape, dim):
    return lax.broadcasted_iota(jnp.int32, shape, dim)


def pick(condition):
    return jnp.where(condition, 1.0, 0.0)


def twelfth(value):
    return (value * 5462) >> 16


SCRATCH = dict(
    buf=((1024, 2048), BF), mwb=((256, 2048), BF), mc=((1024, 256), BF),
    sib_out=((512, 256), BF), sib_in=((512, 256), BF), tgc=((512, 256), BF), tgs=((128, 1024), BF),
    pg=((512, 128), BF), sel=((384, 512), BF),
    outb=((2, 512, 512), BF), inb=((2, 512, 512), BF),
    sc=((1536, 1024), BF), xv=((1536, 1024), BF), wi=((1024, 1024), BF), wo=((1024, 1024), BF),
    hid=((1536, 1024), BF), slope=((1536, 1024), F32), bg=((1536, 1024), BF), rp=((1536, 1024), BF),
    fb=((2, 2, 192, 512), BF), wb=((2, 2, 384, 512), BF),
    sgo=((4, 32, 128), BF), sgi=((4, 32, 128), BF),
    back=((2, 512, 512), BF), ret=((2, 512, 512), BF),
    hogs=((128, 1024), BF), hc=((1024, 256), BF), liv=((1024, 2048), BF), hwv=((2048, 256), BF),
    halves=((10, 2, 16, 2048), BF), wholes=((10, 2, 32, 2048), BF),
    hgo=((4, 1024, 128), BF), hgi=((4, 1024, 128), BF),
    mgo=((4, 128, 1024), BF), mgi=((4, 128, 1024), BF),
)
SEMS = dict(
    og_s=(40,), og_r=(40,), li_s=(40,), li_r=(40,), ig_s=(40,), ig_r=(40,),
    mw_s=(4,), mw_r=(4,), hw_s=(4,), hw_r=(4,),
    mc_s=(16,), mc_r=(16,), tk_s=(16,), tk_r=(16,), hc_s=(16,), hc_r=(16,),
    to_s=(2, 32), to_r=(2, 32), fr_s=(2, 32), fr_r=(2, 32),
    xv_s=(4,), xv_r=(4,), sc_s=(2, 4), sc_r=(2, 4), rp_s=(2, 4), rp_r=(2, 4),
    sg_s=(4,), sg_r=(4,), mg_s=(4,), mg_r=(4,), hg_s=(4,), hg_r=(4,),
    local=(8,), sib_s=(8,), sib_r=(8,),
)
NAMES = list(SCRATCH) + list(SEMS)


class Named:
    def __init__(self, names, refs):
        for name, ref in zip(names, refs, strict=True):
            setattr(self, name, ref)


def kernel(og, mw, merged, disp, w_in, w_out, li, hw, ids, gates,
           ig, hg, mg, ing, outg, gg, *refs):
    v = Named(NAMES, refs)
    me = place()
    z, x, y, c = me
    chip = y * 4 + x
    e = chip * 2 + c
    other = at(z, x, y, 1 - c)

    barrier = pltpu.get_barrier_semaphore()

    def greet(k, _):
        pl.semaphore_signal(
            barrier, inc=1, device_id={"group": z, "expert": lax.rem(e + k, 32)},
            device_id_type=MESH,
        )
        return 0

    lax.fori_loop(1, 32, greet, 0)
    for step in (1, 2, 3):
        for core in (0, 1):
            pl.semaphore_signal(
                barrier, inc=1, device_id=at(wrap(z + step), x, y, core), device_id_type=MESH
            )

    def local(src, dst, k):
        copy = pltpu.make_async_copy(src, dst, v.local.at[k])
        copy.start()
        return copy

    mine = rows(c * 512 + chip * 32, 32)
    theirs = rows((1 - c) * 512 + chip * 32, 32)
    own_half, other_half = lanes(c * 2048, 2048), lanes((1 - c) * 2048, 2048)
    own_rows = rows(384 * z, 384)
    og_load = local(og.at[:, own_half], v.buf.at[mine], 0)
    xv_load = local(disp, v.xv.at[own_rows], 1)
    li_load = local(li.at[:, own_half], v.liv.at[mine], 2)
    wi_load = local(w_in, v.wi, 3)
    wo_load = local(w_out, v.wo, 4)

    names = [pick(iota((32, 128), 0) == ids[k:k + 1, :]) for k in (0, 1)]
    before = pick(iota((128, 128), 0) < iota((128, 128), 1)).astype(BF)
    counts = dot((names[0] + names[1]).astype(BF), before, NN)
    ranks = [jnp.sum(name * counts, axis=0, keepdims=True) for name in names]
    slots = iota((512, 128), 0).astype(F32)
    table = jnp.zeros((512, 128), F32)
    for k in (0, 1):
        target = ids[k:k + 1, :].astype(F32) * 16.0 + ranks[k]
        table = table + jnp.where(slots == target, gates[k:k + 1, :], 0.0)
    source = iota((128, 128), 0)
    order = pick(iota((128, 128), 1) == (source & 3) * 32 + (source >> 2)).astype(BF)
    v.pg[...] = dot(table.astype(BF), order, NN).astype(BF)
    row = iota((384, 512), 0)
    v.sel[...] = pick(iota((384, 512), 1) == row + 4 * twelfth(row)).astype(BF)

    pl.semaphore_wait(barrier, 37)

    send(og.at[:, other_half], v.buf.at[mine], v.sib_s.at[0], v.sib_r.at[0], other)
    weights = Fourfold(
        mw, lambda i, j: v.mwb.at[rows(128 * j, 128), lanes(1024 * i, 1024)], v.mw_s, v.mw_r, me
    )
    weights.start()
    og_load.wait()
    wait(v.buf.at[theirs], v.sib_r.at[0])
    gather = PlaneGather(v.buf, v.og_s, v.og_r, me)
    for h in (0, 1):
        gather.first(h)
    columns = ChipSwap(
        lambda to: merged.at[:, lanes(256 * to, 256)],
        lambda k: v.mc.at[rows(c * 512 + k * 32, 32)],
        v.mc_s, v.mc_r, me,
    )
    columns.start()
    xv_load.wait()
    inputs = DepthGather(v.xv, pl.ds(0, 1024), v.xv_s, v.xv_r, me)
    inputs.start()
    send(li.at[:, other_half], v.liv.at[mine], v.sib_s.at[1], v.sib_r.at[1], other)
    for _ in gather.steps():
        pass
    weights.arrive()

    def product(h, tile):
        return dot(v.buf[rows(h * 512 + tile * 256, 256), :], v.mwb[...], NT)

    for tile in (0, 1):
        v.sib_out[pl.ds(tile * 256, 256), :] = product(1 - c, tile).astype(BF)
    send(v.sib_out, v.sib_in, v.sib_s.at[2], v.sib_r.at[2], other)
    own = [product(c, tile) for tile in (0, 1)]
    wait(v.sib_in, v.sib_r.at[2])
    for tile in (0, 1):
        part = pl.ds(tile * 256, 256)
        v.tgc[part, :] = (own[tile] + v.sib_in[part, :].astype(F32)).astype(BF)
    tokens = ChipSwap(
        lambda to: v.tgc.at[rows(32 * to, 32)],
        lambda k: v.tgs.at[rows(32 * lax.div(k, 4), 32), lanes(256 * lax.rem(k, 4), 256)],
        v.tk_s, v.tk_r, me,
    )
    tokens.start()
    inputs.take(0)
    inputs.take(1)
    columns.arrive()
    mc_half = v.mc.at[rows(c * 512, 512)]
    send(mc_half, mc_half, v.sib_s.at[3], v.sib_r.at[3], other)
    wi_load.wait()

    def early(step):
        def tile(t, _):
            part = rows(384 * wrap(z + step) + 192 * t, 192)
            value, grade = gelu_pair(dot(v.xv[part, :], v.wi[...], NN))
            v.hid[part, :] = value.astype(BF)
            v.slope[part, :] = grade
            return 0

        lax.fori_loop(0, 2, tile, 0)

    early(0)
    tokens.arrive()

    there, spread = [], []
    for p in (0, 1):
        v.outb[p] = dot(v.pg[...], v.tgs[:, 512 * p:512 * p + 512], NN).astype(BF)
        there.append(DeviceSwap(v.outb.at[p], v.inb.at[p], v.to_s.at[p], v.to_r.at[p], z))
        there[p].start()
        spread.append(
            DepthGather(v.sc, pl.ds(512 * p, 512), v.sc_s.at[p], v.sc_r.at[p], me)
        )
    early(1)
    early(3)
    wait(v.mc.at[rows((1 - c) * 512, 512)], v.sib_r.at[3])
    for p in (0, 1):
        there[p].arrive()
        v.sc[own_rows, 512 * p:512 * p + 512] = dot(v.sel[...], v.inb[p], NN).astype(BF)
        spread[p].start()
    li_load.wait()
    wait(v.liv.at[theirs], v.sib_r.at[1])
    gather_li = PlaneGather(v.liv, v.li_s, v.li_r, me)
    for h in (0, 1):
        gather_li.first(h)
    progress = gather_li.steps()
    inputs.finish()
    early(2)
    wo_load.wait()
    block = twelfth(iota((32, 384), 1))
    sums = pick(iota((32, 384), 0) == block).astype(BF)
    tall = iota((384, 128), 0)
    mask = pick(iota((384, 128), 1) == tall - 12 * twelfth(tall))

    def chunk(step):
        q = wrap(z + step)
        part = rows(384 * q, 384)
        grad = dot(v.sc[part, :], v.wo[...], NT)
        column = jnp.sum(grad * v.hid[part, :].astype(F32), axis=1, keepdims=True)
        v.sgo[q] = dot(sums, (column * mask).astype(BF), NN).astype(BF)
        v.bg[part, :] = (grad * v.slope[part, :]).astype(BF)
        if step:
            send(v.sgo.at[q], v.sgi.at[z], v.sg_s.at[step], v.sg_r.at[4 - step], at(q, x, y, c))

    def back_rows(step, p):
        part = rows(384 * wrap(z + step), 384)
        v.rp[part, 512 * p:512 * p + 512] = dot(
            v.bg[part, :], v.wi[512 * p:512 * p + 512, :], NT
        ).astype(BF)

    chunk(0)
    next(progress)
    for p in (0, 1):
        spread[p].take(0)
        spread[p].take(1)
    for p in (0, 1):
        back_rows(0, p)
    next(progress)
    for step in (1, 3):
        chunk(step)
        for p in (0, 1):
            back_rows(step, p)
    next(progress)
    for p in (0, 1):
        spread[p].finish()
    chunk(2)
    gathered = [
        DepthScatter(v.rp, pl.ds(512 * p, 512), v.fb.at[p], v.wb.at[p], v.rp_s.at[p], v.rp_r.at[p],
                     me)
        for p in (0, 1)
    ]
    for p in (0, 1):
        back_rows(2, p)
        gathered[p].open()
    next(progress)
    for p in (0, 1):
        gathered[p].middle()
    next(progress)

    def weight(t, _):
        part = lanes(256 * t, 256)
        ing[:, part] = dot(v.xv[...], v.bg[:, part], TN).astype(BF)
        outg[:, part] = dot(v.hid[...], v.sc[:, part], TN).astype(BF)
        return 0

    lax.fori_loop(0, 4, weight, 0)
    for tile in range(4):
        total = dot(v.mc[...], v.buf[:, tile * 512:tile * 512 + 512], TN).astype(BF)
        for j in (0, 1):
            v.mgo[(tile // 2) * 2 + j, :, (tile % 2) * 512:(tile % 2) * 512 + 512] = total[
                128 * j:128 * j + 128
            ]
    for step in (1, 2, 3):
        wait(v.sgi.at[wrap(z + step)], v.sg_r.at[step])
    marks = v.sgo[z].astype(F32)
    for step in (1, 2, 3):
        marks = marks + v.sgi[wrap(z + step)].astype(F32)
    last = pick(iota((512, 32), 0) == iota((512, 32), 1) * 16 + 12).astype(BF)
    marks = dot(last, marks.astype(BF), NN)
    home = []
    for p in (0, 1):
        v.back[p] = dot(v.sel[...], gathered[p].close(), TN).astype(BF)
        if p == 0:
            v.back[0, :, 0:128] = (v.back[0, :, 0:128].astype(F32) + marks).astype(BF)
        home.append(DeviceSwap(v.back.at[p], v.ret.at[p], v.fr_s.at[p], v.fr_r.at[p], z))
        home[p].start()
    head_weights = Fourfold(
        hw, lambda i, j: v.hwv.at[rows(1024 * i, 1024), lanes(128 * j, 128)], v.hw_s, v.hw_r, me
    )
    head_weights.start()
    merge_sum = Fold(v.mgo, v.mgi, v.mg_s, v.mg_r, me)
    for i in (0, 1):
        for j in (0, 1):
            merge_sum.start(i, j)
    for _ in progress:
        pass

    for p in (0, 1):
        home[p].arrive()
        v.hogs[:, 512 * p:512 * p + 512] = dot(v.pg[...], v.ret[p], TN).astype(BF)
    hog_columns = ChipSwap(
        lambda to: v.hogs.at[rows(32 * lax.div(to, 4), 32), lanes(256 * lax.rem(to, 4), 256)],
        lambda k: v.hc.at[rows(c * 512 + k * 32, 32)],
        v.hc_s, v.hc_r, me,
    )
    hog_columns.start()
    found = dot(last, v.ret[0, :, 0:128], TN).astype(BF)
    for k in (0, 1):
        value = dot(found, names[k].astype(BF), TN)
        value = jnp.where(iota((128, 128), 0).astype(F32) == ranks[k], value, 0.0)
        gg[k:k + 1, :] = jnp.sum(value, axis=0, keepdims=True) / gates[k:k + 1, :]
    head_weights.arrive()
    hog_columns.arrive()
    hc_half = v.hc.at[rows(c * 512, 512)]
    send(hc_half, hc_half, v.sib_s.at[4], v.sib_r.at[4], other)

    def product_out(h):
        def step(t, _):
            tile = rows(h * 512 + 128 * t, 128)
            v.buf[tile, :] = dot(v.hc[tile, :], v.hwv[...], NT).astype(BF)
            return 0

        lax.fori_loop(0, 4, step, 0)

    product_out(c)
    wait(v.hc.at[rows((1 - c) * 512, 512)], v.sib_r.at[4])
    product_out(1 - c)
    scatter = PlaneScatter(v.buf, v.halves, v.wholes, v.ig_s, v.ig_r, me)
    scatter.begin_all()
    head_sum = Fold(v.hgo, v.hgi, v.hg_s, v.hg_r, me)
    for i in (0, 1):
        for tile in (0, 1):
            first = i * 1024 + tile * 512
            total = dot(v.liv[:, first:first + 512], v.hc[...], TN)
            for j in (0, 1):
                v.hgo[i * 2 + j, tile * 512:tile * 512 + 512, :] = total[
                    :, 128 * j:128 * j + 128
                ].astype(BF)
        for j in (0, 1):
            head_sum.start(i, j)
    scatter.run()
    give, keep = v.buf.at[theirs], v.buf.at[mine]
    send(give, ig.at[:, own_half], v.sib_s.at[5], v.sib_r.at[5], other)
    ig_keep = local(keep, ig.at[:, own_half], 5)
    merge_sum.arrive()
    mg[...] = (v.mgi[0].astype(F32) + v.mgi[1].astype(F32)) + (
        v.mgi[2].astype(F32) + v.mgi[3].astype(F32)
    )
    head_sum.arrive()
    hg[...] = (v.hgi[0].astype(F32) + v.hgi[1].astype(F32)) + (
        v.hgi[2].astype(F32) + v.hgi[3].astype(F32)
    )
    wait(ig.at[:, other_half], v.sib_r.at[5])
    ig_keep.wait()
    for part in (weights, columns, inputs, tokens, *there, *spread, *gathered, *home,
                 head_weights, merge_sum, hog_columns, head_sum, scatter):
        part.done()
    for step in (1, 2, 3):
        wait(v.sgo.at[wrap(z + step)], v.sg_s.at[step])
    for k, ref in enumerate((v.buf.at[mine], v.liv.at[mine], v.sib_out, mc_half, hc_half, give)):
        wait(ref, v.sib_s.at[k])


VM = pl.BlockSpec(memory_space=pltpu.VMEM)
ANY = pl.BlockSpec(memory_space=pl.ANY)


def body(
    layer_input, out_grad, merged, head_weight, merge_weight,
    expert_in, expert_out, dispatched, expert_ids, gate_values,
):
    outs = (
        ((32, 4096), BF), ((1024, 128), F32), ((128, 1024), F32),
        ((1024, 1024), BF), ((1024, 1024), BF), ((2, 128), F32),
    )
    input_total, head_grad, merge_grad, in_grad, out_weight_grad, gate_grad = pl.pallas_call(
        kernel,
        out_shape=[jax.ShapeDtypeStruct(shape, kind) for shape, kind in outs],
        in_specs=[ANY] * 8 + [VM] * 2,
        out_specs=[VM] * 6,
        scratch_shapes=[pltpu.VMEM(*kind) for kind in SCRATCH.values()]
        + [dma(*shape) for shape in SEMS.values()],
        compiler_params=pltpu.CompilerParams(
            has_side_effects=True, collective_id=0, vmem_limit_bytes=LIMIT
        ),
        cost_estimate=pl.CostEstimate(flops=1 << 35, bytes_accessed=1 << 25, transcendentals=0),
    )(
        out_grad, merge_weight, merged, dispatched[0], expert_in[0], expert_out[0],
        layer_input, head_weight, expert_ids.T, gate_values.T.astype(F32),
    )
    return (
        input_total,
        head_grad,
        merge_grad,
        in_grad[None].astype(F32),
        out_weight_grad[None].astype(F32),
        gate_grad.T.astype(BF),
    )


def solution(mesh):
    placed = (
        P(("group", "expert"), None),
        P(("group", "expert"), None),
        P(("group", "expert"), None),
        P("group", "expert"),
        P("expert", "group"),
        P("expert", None, "group"),
        P("expert", "group", None),
        P("expert", "group", None),
        P(("group", "expert"), None),
        P(("group", "expert"), None),
    )
    return jax.shard_map(
        body,
        mesh=mesh,
        in_specs=placed,
        out_specs=(
            P(("group", "expert"), None),
            P("group", "expert"),
            P("expert", "group"),
            P("expert", None, "group"),
            P("expert", "group", None),
            P(("group", "expert"), None),
        ),
        check_vma=False,
    )
```

time: 257 us -> 182 us (0.71)
  Pallas kernels: 226 us -> 170 us
  local copies, waits for them, and re-layouts: 24.8 us -> 2.3 us
  other arithmetic: 5.47 us -> 9.18 us
    pallas_call x3 -> x1, Pallas kernels: 226 us -> 170 us  [body(): pl.pallas_call(kernel, out_shape=[jax.ShapeDtypeStruct(shape, kind) for s...]
    unnamed x28 -> x9, local copies, waits for them, and re-layouts: 22.1 us -> 2.3 us
    convert_element_type x7 -> x3, other arithmetic: 4.02 us -> 9.18 us  [the longest x1 6.76 us: body(): out_weight_grad[None].astype(F32)]
where the time goes in v2:
time: 182 us
  Pallas kernels  170 us (93%)
  other arithmetic  9.18 us (5%)
  local copies, waits for them, and re-layouts  2.3 us (1%)
    pallas_call x1, Pallas kernels, body(): pl.pallas_call(kernel, out_shape=[jax.ShapeDtypeStruct(shape, kind) for s...  170 us
    convert_element_type x1, other arithmetic, body(): out_weight_grad[None].astype(F32)  6.76 us

profile of v2, /device:TPU:1, one launch (start us, length us, event | category | flops | bytes accessed | tf_op | source)
XLA Modules:
  0.0 182.0 jit_solution(10811927602866853060)
XLA Ops:
  0.6 1.2 convert_bitcast_fusion.gates
  1.9 169.9 %shard_map.145 = (bf16[32,4096]{1,0:T(8,128)(2,1)}, f32[1024,128]{1,0:T(8,128)}, f32[128,1024]{1,0:T(8,128)}, bf16[1024,1024]{1,0:T(8,128)(2,1)}, bf16[1024,1024]{1,0:T(8,128)(2,1)}, /*index=5*/f32[2,128]{1,0:T(2,128)}) custom-call(bf16[32,4096]{1,0:T(8,128)(2,1)} %og.1, bf16[128,1024]{1,0:T(8,128)(2,1)} %mw.1, bf16[32,4096]{1,0:T(8,128)(2,1)} %merged.1, ...), custom_call_target="tpu_custom_call" | custom-call | flops 34359738368 | bytes 33554432 | tf_op jit(solution)/shard_map/pallas_call | solution.py:793
  171.8 1.2 convert_bitcast_fusion.1
  173.0 0.0 copy-start.2
  173.0 0.0 copy-start.1
  173.0 0.0 copy-start
  173.0 6.8 %bitcast_convert_fusion = (f32[1,1024,1024]{2,1,0:T(8,128)}, f32[1,1024,1024]{2,1,0:T(8,128)}) fusion(bf16[1024,1024]{1,0:T(8,128)(2,1)} %get-tuple-element.16, bf16[1024,1024]{1,0:T(8,128)(2,1)} %get-tuple-element.15), kind=kLoop, calls=%fused_computation | loop fusion | flops 2097152 | bytes 12582912 | tf_op jit(solution)/shard_map/convert_element_type | solution.py:813
  179.7 0.0 copy-done.2
  179.7 0.7 copy.19
  180.4 0.0 copy-done.1
  180.4 0.8 copy.20
  181.2 0.0 copy-done
  181.2 0.8 copy.21
Async XLA Ops:
  173.0 6.8 %copy-start.2 = (bf16[32,4096]{1,0:T(8,128)(2,1)S(1)}, bf16[32,4096]{1,0:T(8,128)(2,1)}, u32[]{:S(2)}) copy-start(bf16[32,4096]{1,0:T(8,128)(2,1)} %get-tuple-element.26) | copy-start | bytes 786436
  173.0 7.5 %copy-start.1 = (f32[1024,128]{1,0:T(8,128)S(1)}, f32[1024,128]{1,0:T(8,128)}, u32[]{:S(2)}) copy-start(f32[1024,128]{1,0:T(8,128)} %get-tuple-element.27) | copy-start | bytes 1572868
  173.0 8.3 %copy-start = (f32[128,1024]{1,0:T(8,128)S(1)}, f32[128,1024]{1,0:T(8,128)}, u32[]{:S(2)}) copy-start(f32[128,1024]{1,0:T(8,128)} %get-tuple-element.28) | copy-start | bytes 1572868

commit v3 on v2

v3 whole, which is shorter than its diff:
```python
import jax
import jax.numpy as jnp
from jax import lax
from jax.experimental import pallas as pl
from jax.experimental.pallas import tpu as pltpu
from jax.sharding import PartitionSpec as P

MESH = pl.DeviceIdType.MESH
BF = jnp.bfloat16
F32 = jnp.float32
LIMIT = 63 << 20

root_scale = 0.7978845608028654
cubic_term = 0.044715


def gelu_pair(value):
    square = value * value
    tangent = jnp.tanh(root_scale * value * (1.0 + cubic_term * square))
    half = 0.5 * (1.0 + tangent)
    slope = half + 0.5 * value * (1.0 - tangent * tangent) * root_scale * (
        1.0 + 3.0 * cubic_term * square
    )
    return value * half, slope


def dot(left, right, dims):
    return lax.dot_general(left, right, ((dims[:1], dims[1:]), ((), ())), preferred_element_type=F32)


NN, NT, TN = (1, 0), (1, 1), (0, 0)


def wrap(value):
    return lax.rem(value + 8, 4)


def place():
    e = lax.axis_index("expert")
    return lax.axis_index("group"), lax.rem(lax.div(e, 2), 4), lax.div(e, 8), lax.rem(e, 2)


def at(z, x, y, c):
    return {"group": z, "expert": (y * 4 + x) * 2 + c}


def by_chip(z, chip, c):
    return {"group": z, "expert": chip * 2 + c}


def rows(start, size):
    return pl.ds(pl.multiple_of(start, 16), size)


def lanes(start, size):
    return pl.ds(pl.multiple_of(start, 128), size)


def send(src, dst, ss, rs, device):
    pltpu.make_async_remote_copy(
        src_ref=src, dst_ref=dst, send_sem=ss, recv_sem=rs, device_id=device, device_id_type=MESH
    ).start()


def wait(ref, sem):
    pltpu.make_async_copy(ref, ref, sem).wait()


class PlaneGather:
    def __init__(self, buf, base, ss, rs, me):
        self.buf, self.base, self.ss, self.rs, self.me = buf, base, ss, rs, me

    def shift(self, h, i, j):
        z, x, y, c = self.me
        dx, dy = (i, j) if h == 0 else (j, i)
        return wrap(x + dx), wrap(y + dy)

    def piece(self, h, spot, half=None):
        px, py = self.shift(h, *spot)
        row = self.base + (py * 4 + px) * 32 + h * 16
        if half is None:
            return self.buf.at[rows(row, 16)]
        return self.buf.at[rows(row, 16), half * 1024:half * 1024 + 1024]

    def spot(self, stage, i, j):
        return (j, 0) if stage == 0 else (i, j)

    def ring(self, h, stage, i):
        return h * 5 + (0 if stage == 0 else 1 + i % 4)

    def sem(self, h, stage, i, kind):
        return self.rs.at[self.ring(h, stage, i) * 3 + min(kind, 2)]

    def post(self, ref, dst, h, stage, i, kind, step):
        px, py = self.shift(h, *((step, 0) if stage == 0 else (0, step)))
        send(ref, dst, self.ss, self.sem(h, stage, i, kind), at(self.me[0], px, py, self.me[3]))

    def begin(self, h, stage, i=0):
        ref = self.piece(h, self.spot(stage, i, 0))
        self.post(ref, ref, h, stage, i, 0, 1)
        self.post(ref, ref, h, stage, i, 1, -1)

    def take(self, h, stage, i, kind):
        spot = self.spot(stage, i, (-1, 1)[kind])
        wait(self.piece(h, spot), self.sem(h, stage, i, kind))
        ref = self.piece(h, spot, kind)
        self.post(ref, ref, h, stage, i, kind + 2, (1, -1)[kind])

    def relay(self, h, stage, i=0):
        self.take(h, stage, i, 0)
        self.take(h, stage, i, 1)

    def close(self, h, stage, i=0):
        wait(self.piece(h, self.spot(stage, i, 2)), self.sem(h, stage, i, 2))

    def first(self):
        for h in (0, 1):
            self.begin(h, 0)
            self.begin(h, 1, 0)

    def steps(self):
        for h in (0, 1):
            self.take(h, 0, 0, 0)
            self.begin(h, 1, -1)
            self.take(h, 0, 0, 1)
            self.begin(h, 1, 1)
        yield
        for h in (0, 1):
            self.relay(h, 1, 0)
        for h in (0, 1):
            self.close(h, 0)
            self.begin(h, 1, 2)
        yield
        for i in (-1, 1):
            for h in (0, 1):
                self.relay(h, 1, i)
            yield
        for h in (0, 1):
            self.relay(h, 1, 2)
        yield

    def finish(self):
        for i in (0, -1, 1, 2):
            for h in (0, 1):
                self.close(h, 1, i)

    def done(self):
        wait(self.buf.at[self.base:self.base + 480], self.ss)


class PlaneScatter(PlaneGather):
    def __init__(self, buf, base, halves, wholes, ss, rs, me):
        super().__init__(buf, base, ss, rs, me)
        self.halves, self.wholes = halves, wholes

    def sem(self, h, stage, i, kind):
        return self.rs.at[self.ring(h, stage, i) * 2 + kind // 2]

    def open(self, h, stage, i=0):
        r = self.ring(h, stage, i)
        for kind, step in ((0, 1), (1, -1)):
            ref = self.piece(h, self.spot(stage, i, 2), kind)
            self.post(ref, self.halves.at[r, kind], h, stage, i, kind, step)

    def middle(self, h, stage, i=0):
        r = self.ring(h, stage, i)
        wait(self.halves.at[r], self.sem(h, stage, i, 0))
        for kind, step in ((0, 1), (1, -1)):
            got = self.halves.at[r, kind]
            own = self.piece(h, self.spot(stage, i, step), kind)
            own[...] = (own[...].astype(F32) + got[...].astype(F32)).astype(BF)
            ref = self.piece(h, self.spot(stage, i, step))
            self.post(ref, self.wholes.at[r, kind], h, stage, i, kind + 2, step)

    def add(self, h, stage, i=0):
        r = self.ring(h, stage, i)
        wait(self.wholes.at[r], self.sem(h, stage, i, 2))
        own = self.piece(h, self.spot(stage, i, 0))
        own[...] = (
            own[...].astype(F32)
            + self.wholes[r, 0].astype(F32)
            + self.wholes[r, 1].astype(F32)
        ).astype(BF)

    def first(self):
        for i in (2, -1, 1, 0):
            for h in (0, 1):
                self.open(h, 1, i)

    def steps(self):
        for i in (2, -1, 1, 0):
            for h in (0, 1):
                self.middle(h, 1, i)
        yield
        for h in (0, 1):
            self.add(h, 1, 2)
            self.open(h, 0)
        for i in (-1, 1):
            for h in (0, 1):
                self.add(h, 1, i)
        yield
        for h in (0, 1):
            self.middle(h, 0)
        for h in (0, 1):
            self.add(h, 1, 0)
        yield
        for h in (0, 1):
            self.add(h, 0)
        yield


class Fourfold:
    def __init__(self, src, slot, dst, ss, rs, me):
        self.src, self.slot, self.dst, self.ss, self.rs, self.me = src, slot, dst, ss, rs, me
        z, x, y, c = me
        self.core = lax.div(z, 2)
        self.own = self.core == c

    def start(self):
        z, x, y, c = self.me
        dst = self.slot(lax.rem(z, 2), c)
        @pl.when(self.own)
        def _():
            pltpu.make_async_copy(self.src, dst, self.rs).start()

        @pl.when(jnp.logical_not(self.own))
        def _():
            send(self.src, dst, self.ss.at[1], self.rs, at(z, x, y, self.core))

        for k in (1, 3, 2):
            send(self.src, dst, self.ss.at[0], self.rs, at(wrap(z + k), x, y, self.core))

    def arrive(self):
        wait(self.dst, self.rs)

    def done(self):
        @pl.when(jnp.logical_not(self.own))
        def _():
            wait(self.src, self.ss.at[1])

        wait(self.dst.at[0:self.dst.shape[0] * 3 // 4], self.ss.at[0])


class Fold:
    def __init__(self, out, got, ss, rs, me):
        self.out, self.got, self.ss, self.rs, self.me = out, got, ss, rs, me

    def start(self, i, j):
        z, x, y, c = self.me
        p = i * 2 + j
        to = 2 * c + i
        own = jnp.logical_and(to == z, c == j)

        @pl.when(own)
        def _():
            pltpu.make_async_copy(self.out.at[p], self.got.at[z], self.rs).start()

        @pl.when(jnp.logical_not(own))
        def _():
            send(self.out.at[p], self.got.at[z], self.ss, self.rs, at(to, x, y, j))

    def arrive(self):
        wait(self.got, self.rs)

    def done(self):
        z, x, y, c = self.me
        own = lax.div(z, 2) == c

        @pl.when(own)
        def _():
            wait(self.out.at[0:3], self.ss)

        @pl.when(jnp.logical_not(own))
        def _():
            wait(self.out, self.ss)


class ChipSwap:
    def __init__(self, src, dst, size, ss, rs, me):
        self.src, self.dst, self.size, self.ss, self.rs, self.me = src, dst, size, ss, rs, me
        self.chip = me[2] * 4 + me[1]

    def start(self):
        z, x, y, c = self.me
        mine = self.chip

        def step(k, _):
            to = lax.rem(mine + k, 16)
            send(self.src(to), self.dst(mine), self.ss, self.rs, by_chip(z, to, c))
            return 0

        pltpu.make_async_copy(self.src(mine), self.dst(mine), self.rs).start()
        lax.fori_loop(1, 16, step, 0)

    def arrive(self):
        wait(self.size.at[0:512], self.rs)

    def done(self):
        wait(self.size.at[0:480], self.ss)


class Dispatch:
    def __init__(self, out, got, ss, rs, me):
        self.out, self.got, self.ss, self.rs, self.me = out, got, ss, rs, me
        self.chip = me[2] * 4 + me[1]
        self.e = self.chip * 2 + me[3]

    def start(self):
        dst, sem = self.got.at[rows(16 * self.chip, 16)], self.rs

        def step(k, _):
            to = lax.rem(self.e + k, 32)
            send(self.out.at[rows(16 * to, 16)], dst, self.ss, sem,
                 {"group": self.me[0], "expert": to})
            return 0

        pltpu.make_async_copy(self.out.at[rows(16 * self.e, 16)], dst, sem).start()
        lax.fori_loop(1, 32, step, 0)

    def arrive(self):
        wait(self.got, self.rs)


class Return:
    def __init__(self, out, got, half, ss, rs, me):
        self.out, self.got, self.half, self.ss, self.rs, self.me = out, got, half, ss, rs, me
        self.chip = me[2] * 4 + me[1]
        self.e = self.chip * 2 + me[3]

    def start(self):
        dst, sem = self.got.at[rows(16 * self.e, 16)], self.rs

        def step(k, _):
            to = lax.rem(self.chip + k, 16)
            send(self.out.at[rows(16 * to, 16)], dst, self.ss.at[0], sem,
                 by_chip(self.me[0], to, self.half))
            return 0

        lax.fori_loop(1, 16, step, 0)
        own = self.out.at[rows(16 * self.chip, 16)]

        @pl.when(self.me[3] == self.half)
        def _():
            pltpu.make_async_copy(own, dst, sem).start()

        @pl.when(self.me[3] != self.half)
        def _():
            send(own, dst, self.ss.at[1], sem, by_chip(self.me[0], self.chip, self.half))

    def arrive(self):
        wait(self.got, self.rs)

    def done(self):
        wait(self.out.at[0:240], self.ss.at[0])

        @pl.when(self.me[3] != self.half)
        def _():
            wait(self.out.at[0:16], self.ss.at[1])


class DepthGather:
    def __init__(self, buf, base, size, ss, rs, me):
        self.buf, self.base, self.size, self.ss, self.rs, self.me = buf, base, size, ss, rs, me

    def piece(self, step, half=None):
        row = 384 * wrap(self.me[0] + step) + self.base
        if half is None:
            return self.buf.at[rows(row, self.size)]
        return self.buf.at[rows(row + self.size // 2 * half, self.size // 2)]

    def to(self, step):
        z, x, y, c = self.me
        return at(wrap(z + step), x, y, c)

    def start(self):
        own = self.piece(0)
        send(own, own, self.ss, self.rs.at[0], self.to(1))
        send(own, own, self.ss, self.rs.at[1], self.to(-1))

    def take(self):
        for kind, step in ((0, -1), (1, 1)):
            wait(self.piece(step), self.rs.at[kind])
            half = self.piece(step, kind)
            send(half, half, self.ss, self.rs.at[2], self.to(-step))

    def finish(self):
        wait(self.piece(2), self.rs.at[2])

    def done(self):
        wait(self.buf.at[0:3 * self.size], self.ss)


class DepthScatter(DepthGather):
    def __init__(self, buf, base, size, halves, wholes, ss, rs, me):
        super().__init__(buf, base, size, ss, rs, me)
        self.halves, self.wholes = halves, wholes

    def open(self):
        for kind, step in ((0, 1), (1, -1)):
            send(self.piece(2, kind), self.halves.at[kind], self.ss, self.rs.at[0], self.to(step))

    def middle(self):
        wait(self.halves, self.rs.at[0])
        for kind, step in ((0, 1), (1, -1)):
            own = self.piece(step, kind)
            own[...] = (own[...].astype(F32) + self.halves[kind].astype(F32)).astype(BF)
            send(self.piece(step), self.wholes.at[kind], self.ss, self.rs.at[1], self.to(step))

    def total(self):
        wait(self.wholes, self.rs.at[1])
        return (
            self.piece(0)[...].astype(F32)
            + self.wholes[0].astype(F32)
            + self.wholes[1].astype(F32)
        ).astype(BF)


def dma(*shape):
    return pltpu.SemaphoreType.DMA(shape)


def iota(shape, dim):
    return lax.broadcasted_iota(jnp.int32, shape, dim)


def pick(condition):
    return jnp.where(condition, 1.0, 0.0)


def twelfth(value):
    return (value * 5462) >> 16


SCRATCH = dict(
    buf=((1024, 2048), BF), mwb=((256, 2048), BF), mc=((1024, 256), BF),
    sib_out=((512, 256), BF), sib_in=((512, 256), BF), tgc=((512, 256), BF), tgs=((128, 1024), BF),
    pg=((512, 128), BF), sel=((192, 256), BF),
    outb=((512, 1024), BF), inb=((2, 256, 1024), BF),
    sc=((1536, 1024), BF), xv=((1536, 1024), BF), wi=((1024, 1024), BF), wo=((1024, 1024), BF),
    hid=((1536, 1024), BF), slope=((1536, 1024), F32), bg=((1536, 1024), BF), rp=((1536, 1024), BF),
    fb=((2, 2, 96, 1024), BF), wb=((2, 2, 192, 1024), BF),
    sgo=((2, 4, 16, 128), BF), sgi=((2, 4, 16, 128), BF),
    back=((2, 256, 1024), BF), ret=((512, 1024), BF),
    hogs=((128, 1024), BF), hc=((1024, 256), BF), liv=((1024, 2048), BF), hwv=((2048, 256), BF),
    halves=((2, 10, 2, 16, 1024), BF), wholes=((2, 10, 2, 16, 2048), BF),
    hgo=((4, 1024, 128), BF), hgi=((4, 1024, 128), BF),
    mgo=((4, 128, 1024), BF), mgi=((4, 128, 1024), BF),
    ingv=((1024, 1024), BF), outgv=((1024, 1024), BF),
)
SEMS = dict(
    og_s=(2,), og_r=(2, 30), li_s=(2,), li_r=(2, 30), ig_s=(2,), ig_r=(2, 20),
    mw_s=(2,), mw_r=(1,), hw_s=(2,), hw_r=(1,),
    mc_s=(1,), mc_r=(1,), tk_s=(1,), tk_r=(1,), hc_s=(1,), hc_r=(1,),
    to_s=(1,), to_r=(2,), fr_s=(2, 2), fr_r=(1,),
    xv_s=(1,), xv_r=(3,), sc_s=(2,), sc_r=(2, 3), rp_s=(2,), rp_r=(2, 2),
    sg_s=(2,), sg_r=(2,), mg_s=(1,), mg_r=(1,), hg_s=(1,), hg_r=(1,),
    local=(6,), out=(2,), sib_s=(6,), sib_r=(6,),
)
NAMES = list(SCRATCH) + list(SEMS)


class Named:
    def __init__(self, names, refs):
        for name, ref in zip(names, refs, strict=True):
            setattr(self, name, ref)


def kernel(og, mw, merged, disp, w_in, w_out, li, hw, ids, gates,
           ig, hg, mg, ing, outg, gg, *refs):
    v = Named(NAMES, refs)
    me = place()
    z, x, y, c = me
    chip = y * 4 + x
    e = chip * 2 + c
    other = at(z, x, y, 1 - c)

    barrier = pltpu.get_barrier_semaphore()

    def greet(k, _):
        pl.semaphore_signal(
            barrier, inc=1, device_id={"group": z, "expert": lax.rem(e + k, 32)},
            device_id_type=MESH,
        )
        return 0

    lax.fori_loop(1, 32, greet, 0)
    for step in (1, 2, 3):
        for core in (0, 1):
            pl.semaphore_signal(
                barrier, inc=1, device_id=at(wrap(z + step), x, y, core), device_id_type=MESH
            )

    def local(src, dst, k):
        copy = pltpu.make_async_copy(src, dst, v.local.at[k])
        copy.start()
        return copy

    mine = rows(c * 512 + chip * 32, 32)
    theirs = rows((1 - c) * 512 + chip * 32, 32)
    own_half, other_half = lanes(c * 2048, 2048), lanes((1 - c) * 2048, 2048)
    own_rows = rows(384 * z, 384)
    raw = v.rp.at[0:384]
    xv_load = local(disp, raw, 1)
    og_load = local(og.at[:, own_half], v.buf.at[mine], 0)
    wi_load = local(w_in, v.wi, 3)
    li_load = local(li.at[:, own_half], v.liv.at[mine], 2)
    wo_load = local(w_out, v.wo, 4)

    row = iota((384, 384), 0)
    late = (row >= 192).astype(jnp.int32)
    first = row - 192 * late
    order = pick(iota((384, 384), 1) == first + 12 * twelfth(first) + 12 * late).astype(BF)
    xv_load.wait()
    v.xv[own_rows, :] = dot(order, raw[...], NN).astype(BF)
    pl.semaphore_wait(barrier, 37)

    send(og.at[:, other_half], v.buf.at[mine], v.sib_s.at[0], v.sib_r.at[0], other)
    weights = Fourfold(
        mw, lambda i, j: v.mwb.at[rows(128 * j, 128), lanes(1024 * i, 1024)], v.mwb,
        v.mw_s, v.mw_r.at[0], me,
    )
    weights.start()
    gather = [PlaneGather(v.buf, 512 * h, v.og_s.at[h], v.og_r.at[h], me) for h in (0, 1)]
    gather_li = [PlaneGather(v.liv, 512 * h, v.li_s.at[h], v.li_r.at[h], me) for h in (0, 1)]
    og_load.wait()
    wait(v.buf.at[theirs], v.sib_r.at[0])
    gather[0].first()

    names = [pick(iota((32, 128), 0) == ids[k:k + 1, :]) for k in (0, 1)]
    before = pick(iota((128, 128), 0) < iota((128, 128), 1)).astype(BF)
    counts = dot((names[0] + names[1]).astype(BF), before, NN)
    ranks = [jnp.sum(name * counts, axis=0, keepdims=True) for name in names]
    values = gates[...].astype(F32)
    slots = iota((512, 128), 0).astype(F32)
    table = jnp.zeros((512, 128), F32)
    for k in (0, 1):
        target = ids[k:k + 1, :].astype(F32) * 16.0 + ranks[k]
        table = table + jnp.where(slots == target, values[k:k + 1, :], 0.0)
    source = iota((128, 128), 0)
    order = pick(iota((128, 128), 1) == (source & 3) * 32 + (source >> 2)).astype(BF)
    v.pg[...] = dot(table.astype(BF), order, NN).astype(BF)
    row = iota((192, 256), 0)
    v.sel[...] = pick(iota((192, 256), 1) == row + 4 * twelfth(row)).astype(BF)
    block = twelfth(iota((16, 192), 1))
    sums = pick(iota((16, 192), 0) == block).astype(BF)
    tall = iota((192, 128), 0)
    mask = pick(iota((192, 128), 1) == tall - 12 * twelfth(tall))
    last = pick(iota((512, 32), 0) == iota((512, 32), 1) * 16 + 12).astype(BF)
    last_half = pick(iota((256, 16), 0) == iota((256, 16), 1) * 16 + 12).astype(BF)

    inputs = DepthGather(v.xv, 0, 384, v.xv_s.at[0], v.xv_r, me)

    def early(step, h):
        part = rows(384 * wrap(z + step) + 192 * h, 192)
        value, grade = gelu_pair(dot(v.xv[part, :], v.wi[...], NN))
        v.hid[part, :] = value.astype(BF)
        v.slope[part, :] = grade

    def product(h):
        def tile(t):
            return dot(v.buf[h * 512 + t * 256:h * 512 + t * 256 + 256, :], v.mwb[...], NT)

        @pl.when(c != h)
        def _():
            for t in (0, 1):
                v.sib_out[256 * t:256 * t + 256, :] = tile(t).astype(BF)
            send(v.sib_out, v.sib_in, v.sib_s.at[2], v.sib_r.at[2], other)

        @pl.when(c == h)
        def _():
            own = [tile(t) for t in (0, 1)]
            wait(v.sib_in, v.sib_r.at[2])
            for t in (0, 1):
                part = slice(256 * t, 256 * t + 256)
                v.tgc[part, :] = (own[t] + v.sib_in[part, :].astype(F32)).astype(BF)
            tokens.start()

    tokens = ChipSwap(
        lambda to: v.tgc.at[rows(32 * to, 32)],
        lambda k: v.tgs.at[rows(32 * lax.div(k, 4), 32), lanes(256 * lax.rem(k, 4), 256)],
        v.tgc, v.tk_s.at[0], v.tk_r.at[0], me,
    )
    there = [Dispatch(v.outb, v.inb.at[h], v.to_s.at[0], v.to_r.at[h], me) for h in (0, 1)]
    spread = [DepthGather(v.sc, 192 * h, 192, v.sc_s.at[h], v.sc_r.at[h], me) for h in (0, 1)]

    def dispatch(h):
        @pl.when(c == h)
        def _():
            tokens.arrive()
            for t in (0, 1):
                part = slice(512 * t, 512 * t + 512)
                v.outb[:, part] = dot(v.pg[...], v.tgs[:, part], NN).astype(BF)
            there[h].start()

    def to_experts(h):
        there[h].arrive()
        part = rows(384 * z + 192 * h, 192)
        v.sc[part, :] = dot(v.sel[...], v.inb[h], NN).astype(BF)
        spread[h].start()

    def chunk(h, step):
        q = wrap(z + step)
        part = rows(384 * q + 192 * h, 192)
        grad = dot(v.sc[part, :], v.wo[...], NT)
        column = jnp.sum(grad * v.hid[part, :].astype(F32), axis=1, keepdims=True)
        v.sgo[h, q] = dot(sums, (column * mask).astype(BF), NN).astype(BF)
        v.bg[part, :] = (grad * v.slope[part, :]).astype(BF)
        if step:
            send(v.sgo.at[h, q], v.sgi.at[h, z], v.sg_s.at[h], v.sg_r.at[h],
                 at(q, x, y, c))
        v.rp[part, :] = dot(v.bg[part, :], v.wi[...], NT).astype(BF)

    columns = ChipSwap(
        lambda to: merged.at[:, lanes(256 * to, 256)],
        lambda k: v.mc.at[rows(c * 512 + k * 32, 32)],
        v.mc, v.mc_s.at[0], v.mc_r.at[0], me,
    )
    head_weights = Fourfold(
        hw, lambda i, j: v.hwv.at[rows(1024 * i, 1024), lanes(128 * j, 128)], v.hwv,
        v.hw_s, v.hw_r.at[0], me,
    )
    waves, more = [half.steps() for half in gather]
    next(waves)
    inputs.start()
    send(li.at[:, other_half], v.liv.at[mine], v.sib_s.at[1], v.sib_r.at[1], other)
    next(waves)
    gather[1].first()
    wi_load.wait()
    early(0, 0)
    next(waves)
    early(0, 1)
    next(waves)
    next(waves)
    next(more)
    gather[0].finish()
    weights.arrive()
    product(0)
    next(more)
    next(more)
    dispatch(0)
    inputs.take()
    head_weights.start()
    next(more)
    next(more)
    gather[1].finish()
    product(1)
    to_experts(0)
    early(1, 0)
    early(3, 0)
    dispatch(1)
    inputs.finish()
    early(2, 0)
    wo_load.wait()
    chunk(0, 0)
    to_experts(1)
    columns.start()
    spread[0].take()
    li_load.wait()
    wait(v.liv.at[theirs], v.sib_r.at[1])
    gather_li[0].first()
    li_waves = [half.steps() for half in gather_li]
    chunk(0, 1)
    chunk(0, 3)
    next(li_waves[0])
    early(1, 1)
    spread[0].finish()
    chunk(0, 2)
    back = [
        DepthScatter(v.rp, 192 * h, 192, v.fb.at[h], v.wb.at[h], v.rp_s.at[h], v.rp_r.at[h], me)
        for h in (0, 1)
    ]
    back[0].open()
    early(3, 1)
    early(2, 1)
    spread[1].take()
    next(li_waves[0])
    chunk(1, 0)
    back[0].middle()
    chunk(1, 1)
    chunk(1, 3)
    next(li_waves[0])
    spread[1].finish()
    chunk(1, 2)
    back[1].open()
    for _ in li_waves[0]:
        pass
    gather_li[1].first()
    gather_li[0].finish()
    columns.arrive()
    mc_half = v.mc.at[rows(c * 512, 512)]
    send(mc_half, mc_half, v.sib_s.at[3], v.sib_r.at[3], other)

    def weight(t, _):
        part = lanes(256 * t, 256)
        down = rows(256 * t, 256)
        v.ingv[down, :] = dot(v.xv[:, part], v.bg[...], TN).astype(BF)
        v.outgv[down, :] = dot(v.hid[:, part], v.sc[...], TN).astype(BF)
        pltpu.make_async_copy(v.ingv.at[down], ing.at[down], v.out.at[0]).start()
        pltpu.make_async_copy(v.outgv.at[down], outg.at[down], v.out.at[1]).start()
        return 0

    def marks(h):
        wait(v.sgi.at[h, 0:3], v.sg_r.at[h])
        total = v.sgo[h, z].astype(F32)
        for step in (1, 2, 3):
            total = total + v.sgi[h, wrap(z + step)].astype(F32)
        return dot(last_half, total.astype(BF), NN)

    home = [
        Return(v.back.at[h], v.ret, h, v.fr_s.at[h], v.fr_r.at[0], me) for h in (0, 1)
    ]

    def from_experts(h):
        v.back[h] = dot(v.sel[...], back[h].total(), TN).astype(BF)
        v.back[h, :, 0:128] = (v.back[h, :, 0:128].astype(F32) + marks(h)).astype(BF)
        home[h].start()

    hog_columns = ChipSwap(
        lambda to: v.hogs.at[rows(32 * lax.div(to, 4), 32), lanes(256 * lax.rem(to, 4), 256)],
        lambda k: v.hc.at[rows(c * 512 + k * 32, 32)],
        v.hc, v.hc_s.at[0], v.hc_r.at[0], me,
    )
    hc_half = v.hc.at[rows(c * 512, 512)]

    def to_tokens(h):
        @pl.when(c == h)
        def _():
            home[h].arrive()
            for t in (0, 1):
                part = slice(512 * t, 512 * t + 512)
                v.hogs[:, part] = dot(v.pg[...], v.ret[:, part], TN).astype(BF)
            hog_columns.start()

    def to_columns(h):
        @pl.when(c == h)
        def _():
            hog_columns.arrive()
            send(hc_half, hc_half, v.sib_s.at[4], v.sib_r.at[4], other)

        @pl.when(c != h)
        def _():
            wait(v.hc.at[h * 512:h * 512 + 512], v.sib_r.at[4])

    lax.fori_loop(0, 1, weight, 0)
    back[1].middle()
    next(li_waves[1])
    lax.fori_loop(1, 2, weight, 0)
    from_experts(0)
    next(li_waves[1])
    lax.fori_loop(2, 4, weight, 0)
    next(li_waves[1])
    to_tokens(0)
    for _ in li_waves[1]:
        pass
    from_experts(1)
    wait(v.mc.at[rows((1 - c) * 512, 512)], v.sib_r.at[3])
    merge_sum = Fold(v.mgo, v.mgi, v.mg_s.at[0], v.mg_r.at[0], me)
    for tile in range(4):
        total = dot(v.mc[...], v.buf[:, tile * 512:tile * 512 + 512], TN).astype(BF)
        for j in (0, 1):
            v.mgo[(tile // 2) * 2 + j, :, (tile % 2) * 512:(tile % 2) * 512 + 512] = total[
                128 * j:128 * j + 128
            ]
    for half in gather:
        half.done()
    head_weights.arrive()

    def product_out(h):
        def tile(t, _):
            part = rows(h * 512 + 128 * t, 128)
            v.buf[part, :] = dot(v.hc[part, :], v.hwv[...], NT).astype(BF)
            return 0

        lax.fori_loop(0, 4, tile, 0)

    scatter = [
        PlaneScatter(v.buf, 512 * h, v.halves.at[h], v.wholes.at[h], v.ig_s.at[h], v.ig_r.at[h], me)
        for h in (0, 1)
    ]
    to_columns(0)
    product_out(0)
    scatter[0].first()
    for i in (0, 1):
        for j in (0, 1):
            merge_sum.start(i, j)
    adds = scatter[0].steps()
    next(adds)
    to_tokens(1)
    next(adds)
    to_columns(1)
    product_out(1)
    scatter[1].first()
    gather_li[1].finish()
    head_sum = Fold(v.hgo, v.hgi, v.hg_s.at[0], v.hg_r.at[0], me)
    for i in (0, 1):
        for tile in (0, 1):
            at_lane = i * 1024 + tile * 512
            total = dot(v.liv[:, at_lane:at_lane + 512], v.hc[...], TN)
            for j in (0, 1):
                v.hgo[i * 2 + j, tile * 512:tile * 512 + 512, :] = total[
                    :, 128 * j:128 * j + 128
                ].astype(BF)
        for j in (0, 1):
            head_sum.start(i, j)
    later = scatter[1].steps()
    next(adds)
    next(later)
    next(adds)

    def deliver(h):
        piece = v.buf.at[rows(h * 512 + chip * 32, 32)]

        @pl.when(c == h)
        def _():
            pltpu.make_async_copy(piece, ig.at[:, own_half], v.local.at[5]).start()

        @pl.when(c != h)
        def _():
            send(piece, ig.at[:, own_half], v.sib_s.at[5], v.sib_r.at[5], other)

    deliver(0)
    next(later)
    merge_sum.arrive()
    mg[...] = (v.mgi[0].astype(F32) + v.mgi[1].astype(F32)) + (
        v.mgi[2].astype(F32) + v.mgi[3].astype(F32)
    )
    next(later)
    found = dot(last, v.ret[:, 0:128], TN).astype(BF)
    for k in (0, 1):
        value = dot(found, names[k].astype(BF), TN)
        value = jnp.where(iota((128, 128), 0).astype(F32) == ranks[k], value, 0.0)
        gg[k:k + 1, :] = jnp.sum(value, axis=0, keepdims=True) / values[k:k + 1, :]
    next(later)
    deliver(1)
    head_sum.arrive()
    hg[...] = (v.hgi[0].astype(F32) + v.hgi[1].astype(F32)) + (
        v.hgi[2].astype(F32) + v.hgi[3].astype(F32)
    )
    for part in (weights, columns, inputs, tokens, *spread, *back, *home, *gather_li,
                 head_weights, merge_sum, hog_columns, head_sum, *scatter):
        part.done()

    wait(v.outb.at[0:496], v.to_s.at[0])
    for h in (0, 1):
        wait(v.sgo.at[h, 0:3], v.sg_s.at[h])
    wait(ing, v.out.at[0])
    wait(outg, v.out.at[1])
    for k, ref in enumerate((v.buf.at[mine], v.liv.at[mine], v.sib_out, mc_half, hc_half)):
        wait(ref, v.sib_s.at[k])
    wait(ig.at[:, own_half], v.local.at[5])
    wait(ig.at[:, other_half], v.sib_r.at[5])
    wait(v.buf.at[theirs], v.sib_s.at[5])


def widen_kernel(ig, hg, mg, ing, outg, to_ig, to_hg, to_mg, to_ing, to_outg,
                 narrow, wide, via_ig, via_hg, via_mg, s1, s2, s3, s4):
    through = ((ig, via_ig, to_ig), (hg, via_hg, to_hg), (mg, via_mg, to_mg))
    parts = [(src, dst, slice(256 * t, 256 * t + 256))
             for src, dst in ((ing, to_ing), (outg, to_outg)) for t in range(4)]
    loads = [
        pltpu.make_async_copy(src.at[part], narrow.at[k], s1.at[k])
        for k, (src, _, part) in enumerate(parts)
    ]
    stores = [
        pltpu.make_async_copy(wide.at[k], dst.at[part], s2.at[k])
        for k, (_, dst, part) in enumerate(parts)
    ]
    ins = [pltpu.make_async_copy(src, via, s3.at[k]) for k, (src, via, _) in enumerate(through)]
    outs = [pltpu.make_async_copy(via, dst, s4.at[k]) for k, (_, via, dst) in enumerate(through)]
    for copy in loads + ins:
        copy.start()
    for k in range(8):
        loads[k].wait()
        wide[k] = narrow[k].astype(F32)
        stores[k].start()
    for k in range(3):
        ins[k].wait()
        outs[k].start()
    for copy in stores + outs:
        copy.wait()


VM = pl.BlockSpec(memory_space=pltpu.VMEM)
ANY = pl.BlockSpec(memory_space=pl.ANY)


def body(
    layer_input, out_grad, merged, head_weight, merge_weight,
    expert_in, expert_out, dispatched, expert_ids, gate_values,
):
    outs = (
        ((32, 4096), BF), ((1024, 128), F32), ((128, 1024), F32),
        ((1024, 1024), BF), ((1024, 1024), BF), ((2, 128), F32),
    )
    *results, gate_grad = pl.pallas_call(
        kernel,
        out_shape=[jax.ShapeDtypeStruct(shape, kind) for shape, kind in outs],
        in_specs=[ANY] * 8 + [VM] * 2,
        out_specs=[ANY, VM, VM, ANY, ANY, VM],
        scratch_shapes=[pltpu.VMEM(*kind) for kind in SCRATCH.values()]
        + [dma(*shape) for shape in SEMS.values()],
        compiler_params=pltpu.CompilerParams(
            has_side_effects=True, collective_id=0, vmem_limit_bytes=LIMIT
        ),
        cost_estimate=pl.CostEstimate(flops=1 << 35, bytes_accessed=1 << 25, transcendentals=0),
    )(
        out_grad, merge_weight, merged, dispatched[0], expert_in[0], expert_out[0],
        layer_input, head_weight, expert_ids.T, gate_values.T,
    )
    input_total, head_grad, merge_grad, in_grad, out_weight_grad = pl.pallas_call(
        widen_kernel,
        out_shape=[
            jax.ShapeDtypeStruct(shape, kind)
            for shape, kind in (*outs[:3], ((1024, 1024), F32), ((1024, 1024), F32))
        ],
        in_specs=[ANY] * 5,
        out_specs=[ANY] * 5,
        scratch_shapes=[
            pltpu.VMEM((8, 256, 1024), BF), pltpu.VMEM((8, 256, 1024), F32),
            *[pltpu.VMEM(*kind) for kind in outs[:3]], dma(8), dma(8), dma(3), dma(3),
        ],
        compiler_params=pltpu.CompilerParams(vmem_limit_bytes=LIMIT),
        cost_estimate=pl.CostEstimate(flops=1 << 21, bytes_accessed=1 << 24, transcendentals=0),
    )(*results)
    return (
        input_total,
        head_grad,
        merge_grad,
        in_grad[None],
        out_weight_grad[None],
        gate_grad.T.astype(BF),
    )


def solution(mesh):
    placed = (
        P(("group", "expert"), None),
        P(("group", "expert"), None),
        P(("group", "expert"), None),
        P("group", "expert"),
        P("expert", "group"),
        P("expert", None, "group"),
        P("expert", "group", None),
        P("expert", "group", None),
        P(("group", "expert"), None),
        P(("group", "expert"), None),
    )
    return jax.shard_map(
        body,
        mesh=mesh,
        in_specs=placed,
        out_specs=(
            P(("group", "expert"), None),
            P("group", "expert"),
            P("expert", "group"),
            P("expert", None, "group"),
            P("expert", "group", None),
            P(("group", "expert"), None),
        ),
        check_vma=False,
    )
```

time: 182 us -> 178 us (0.978)
  other arithmetic: 9.18 us -> 1.15 us
  Pallas kernels: 170 us -> 176 us
  local copies, waits for them, and re-layouts: 2.3 us -> 0 us
    convert_element_type x2 -> x0, other arithmetic: 7.98 us -> none  [the longest x1 6.76 us: body(): out_weight_grad[None].astype(F32)]
    pallas_call x0 -> x1, Pallas kernels: none -> 5 us  [body(): pl.pallas_call(widen_kernel, out_shape=[jax.ShapeDtypeStruct(shape, kind)...]
    unnamed x9 -> x0, local copies, waits for them, and re-layouts: 2.3 us -> none
where the time goes in v3:
time: 178 us
  Pallas kernels  176 us (99%)
    pallas_call x1, Pallas kernels, body(): pl.pallas_call(kernel, out_shape=[jax.ShapeDtypeStruct(shape, kind) for s...  171 us
    pallas_call x1, Pallas kernels, body(): pl.pallas_call(widen_kernel, out_shape=[jax.ShapeDtypeStruct(shape, kind)...  5 us

profile of v3, /device:TPU:1, one launch (start us, length us, event | category | flops | bytes accessed | tf_op | source)
XLA Modules:
  0.0 178.0 jit_solution(16336588338110874830)
XLA Ops:
  0.6 171.0 %shard_map.145 = (bf16[32,4096]{1,0:T(8,128)(2,1)}, f32[1024,128]{1,0:T(8,128)}, f32[128,1024]{1,0:T(8,128)}, bf16[1024,1024]{1,0:T(8,128)(2,1)}, bf16[1024,1024]{1,0:T(8,128)(2,1)}, /*index=5*/f32[2,128]{1,0:T(2,128)}) custom-call(bf16[32,4096]{1,0:T(8,128)(2,1)} %og.1, bf16[128,1024]{1,0:T(8,128)(2,1)} %mw.1, bf16[32,4096]{1,0:T(8,128)(2,1)} %merged.1, ...), custom_call_target="tpu_custom_call" | custom-call | flops 34359738368 | bytes 33554432 | tf_op jit(solution)/shard_map/pallas_call | solution.py:895
  171.7 1.1 convert_bitcast_fusion
  172.8 5.0 %shard_map.146 = (bf16[32,4096]{1,0:T(8,128)(2,1)}, f32[1024,128]{1,0:T(8,128)}, f32[128,1024]{1,0:T(8,128)}, f32[1024,1024]{1,0:T(8,128)}, f32[1024,1024]{1,0:T(8,128)}) custom-call(bf16[32,4096]{1,0:T(8,128)(2,1)} %get-tuple-element.17.ig, f32[1024,128]{1,0:T(8,128)} %get-tuple-element.18.hg, f32[128,1024]{1,0:T(8,128)} %get-tuple-element.19.mg, ...), custom_call_target="tpu_custom_call" | custom-call | flops 2097152 | bytes 16777216 | tf_op jit(solution)/shard_map/pallas_call | solution.py:910

commit v4 on v3

--- a/solution.py
+++ b/solution.py
@@ -634,12 +634,12 @@
     next(more)
     gather[0].finish()
     weights.arrive()
+    head_weights.start()
     product(0)
     next(more)
     next(more)
     dispatch(0)
     inputs.take()
-    head_weights.start()
     next(more)
     next(more)
     gather[1].finish()
@@ -658,6 +658,7 @@
     li_load.wait()
     wait(v.liv.at[theirs], v.sib_r.at[1])
     gather_li[0].first()
+    gather_li[1].first()
     li_waves = [half.steps() for half in gather_li]
     chunk(0, 1)
     chunk(0, 3)
@@ -684,7 +685,6 @@
     back[1].open()
     for _ in li_waves[0]:
         pass
-    gather_li[1].first()
     gather_li[0].finish()
     columns.arrive()
     mc_half = v.mc.at[rows(c * 512, 512)]
@@ -825,11 +825,13 @@
         v.mgi[2].astype(F32) + v.mgi[3].astype(F32)
     )
     next(later)
+    shares = []
     found = dot(last, v.ret[:, 0:128], TN).astype(BF)
     for k in (0, 1):
         value = dot(found, names[k].astype(BF), TN)
         value = jnp.where(iota((128, 128), 0).astype(F32) == ranks[k], value, 0.0)
-        gg[k:k + 1, :] = jnp.sum(value, axis=0, keepdims=True) / values[k:k + 1, :]
+        shares.append(jnp.sum(value, axis=0, keepdims=True) / values[k:k + 1, :])
+    gg[...] = jnp.concatenate(shares, axis=0).astype(BF)
     next(later)
     deliver(1)
     head_sum.arrive()
@@ -890,7 +892,7 @@
 ):
     outs = (
         ((32, 4096), BF), ((1024, 128), F32), ((128, 1024), F32),
-        ((1024, 1024), BF), ((1024, 1024), BF), ((2, 128), F32),
+        ((1024, 1024), BF), ((1024, 1024), BF), ((2, 128), BF),
     )
     *results, gate_grad = pl.pallas_call(
         kernel,
@@ -928,7 +930,7 @@
         merge_grad,
         in_grad[None],
         out_weight_grad[None],
-        gate_grad.T.astype(BF),
+        gate_grad.T,
     )
 
 

time: 178 us -> 173 us (0.972)
  Pallas kernels: 176 us -> 172 us
    pallas_call x1, Pallas kernels: 171 us -> 167 us  [body(): pl.pallas_call(kernel, out_shape=[jax.ShapeDtypeStruct(shape, kind) for s...]
where the time goes in v4:
time: 173 us
  Pallas kernels  172 us (99%)
    pallas_call x1, Pallas kernels, body(): pl.pallas_call(kernel, out_shape=[jax.ShapeDtypeStruct(shape, kind) for s...  167 us
    pallas_call x1, Pallas kernels, body(): pl.pallas_call(widen_kernel, out_shape=[jax.ShapeDtypeStruct(shape, kind)...  5 us

profile of v4, /device:TPU:1, one launch (start us, length us, event | category | flops | bytes accessed | tf_op | source)
XLA Modules:
  0.0 173.4 jit_solution(10922748064715573591)
XLA Ops:
  0.6 167.2 %shard_map.145 = (bf16[32,4096]{1,0:T(8,128)(2,1)}, f32[1024,128]{1,0:T(8,128)}, f32[128,1024]{1,0:T(8,128)}, bf16[1024,1024]{1,0:T(8,128)(2,1)}, bf16[1024,1024]{1,0:T(8,128)(2,1)}, /*index=5*/bf16[2,128]{1,0:T(2,128)(2,1)}) custom-call(bf16[32,4096]{1,0:T(8,128)(2,1)} %og.1, bf16[128,1024]{1,0:T(8,128)(2,1)} %mw.1, bf16[32,4096]{1,0:T(8,128)(2,1)} %merged.1, ...), custom_call_target="tpu_custom_call" | custom-call | flops 34359738368 | bytes 33554432 | tf_op jit(solution)/shard_map/pallas_call | solution.py:897
  167.8 0.0 copy-start
  167.8 5.0 %shard_map.146 = (bf16[32,4096]{1,0:T(8,128)(2,1)}, f32[1024,128]{1,0:T(8,128)}, f32[128,1024]{1,0:T(8,128)}, f32[1024,1024]{1,0:T(8,128)}, f32[1024,1024]{1,0:T(8,128)}) custom-call(bf16[32,4096]{1,0:T(8,128)(2,1)} %get-tuple-element.17.ig, f32[1024,128]{1,0:T(8,128)} %get-tuple-element.18.hg, f32[128,1024]{1,0:T(8,128)} %get-tuple-element.19.mg, ...), custom_call_target="tpu_custom_call" | custom-call | flops 2097152 | bytes 16777216 | tf_op jit(solution)/shard_map/pallas_call | solution.py:912
  172.8 0.0 copy-done
  172.8 0.5 copy.17
Async XLA Ops:
  167.8 5.0 %copy-start = (bf16[2,128]{1,0:T(2,128)(2,1)S(1)}, bf16[2,128]{1,0:T(2,128)(2,1)}, u32[]{:S(2)}) copy-start(bf16[2,128]{1,0:T(2,128)(2,1)} %get-tuple-element.27) | copy-start | bytes 1540
